TPU v7x, 128 devices: a whole 4x4x4 slice. The times are simulated.
128 devices in a mesh: ctx: 32 (over y, z_hi, x), wt: 4 (over z_lo, core).
Axes of the slice: x: 4, y: 4, z: 4 (z_hi: 2, z_lo: 2; z = z_hi * 2 + z_lo), core: 2. Of those that a mesh axis runs over, the one named last changes fastest.
Arguments:
- stream: bfloat16 [8192, 2048], P('ctx'), may hold values from -6 to 6
- layer_input: bfloat16 [8192, 256], P('ctx', 'wt'), may hold values from -6 to 6
- out_grad: bfloat16 [8192, 2048], P('ctx'), may hold values from -6 to 6
- doc_lengths: int32 [8], replicated, may hold values from 1 to 4096, 8192 in all
- stretch_slots: int32 [64], replicated, may hold values from 0 to 63, each once
- gain_input: float32 [2048], replicated, may hold values from 0.5 to 1.5
- gain_query: float32 [256], replicated, may hold values from 0.6 to 1.4
- gain_key: float32 [256], replicated, may hold values from 0.6 to 1.4
- w_query: bfloat16 [2048, 2048], P(None, 'wt'), may hold values from -0.125 to 0.125
- w_key: bfloat16 [2048, 512], P(None, 'wt'), may hold values from -0.125 to 0.125
- w_value: bfloat16 [2048, 512], P(None, 'wt'), may hold values from -0.125 to 0.125
- w_attn_out: bfloat16 [2048, 2048], P('wt'), may hold values from -0.5 to 0.5
- gain_attn: float32 [2048], replicated, may hold values from 0.5 to 1.5
- laurel_left: bfloat16 [2048, 64], P(None, 'wt'), may hold values from -0.125 to 0.125
- laurel_right: bfloat16 [64, 2048], P('wt'), may hold values from -0.75 to 0.75
- gain_laurel: float32 [2048], replicated, may hold values from 0.5 to 1.5
- gain_pre_ff: float32 [2048], replicated, may hold values from 0.5 to 1.5
- w_gate: bfloat16 [2048, 8192], P(None, 'wt'), may hold values from -0.125 to 0.125
- w_up: bfloat16 [2048, 8192], P(None, 'wt'), may hold values from -0.125 to 0.125
- w_down: bfloat16 [8192, 2048], P('wt'), may hold values from -0.0625 to 0.0625
- gain_post_ff: float32 [2048], replicated, may hold values from 0.5 to 1.5
- join_gate: bfloat16 [2048, 256], P(None, 'wt'), may hold values from -0.125 to 0.125
- join_proj: bfloat16 [256, 2048], P('wt'), may hold values from -0.375 to 0.375
- gain_join: float32 [2048], replicated, may hold values from 0.5 to 1.5
Outputs:
- layer_out: float32 [8192, 2048], P('ctx')
- stream_grad: float32 [8192, 2048], P('ctx')
- layer_input_grad: float32 [8192, 256], P('ctx', 'wt')
- grad_gain_input: float32 [2048], P('ctx')
- grad_gain_query: float32 [256], P('ctx')
- grad_gain_key: float32 [256], P('ctx')
- grad_w_query: float32 [2048, 2048], P('ctx', 'wt')
- grad_w_key: float32 [2048, 512], P('ctx', 'wt')
- grad_w_value: float32 [2048, 512], P('ctx', 'wt')
- grad_w_attn_out: float32 [2048, 2048], P('wt', 'ctx')
- grad_gain_attn: float32 [2048], P('ctx')
- grad_laurel_left: float32 [2048, 64], P('ctx', 'wt')
- grad_laurel_right: float32 [64, 2048], P('wt', 'ctx')
- grad_gain_laurel: float32 [2048], P('ctx')
- grad_gain_pre_ff: float32 [2048], P('ctx')
- grad_w_gate: float32 [2048, 8192], P('ctx', 'wt')
- grad_w_up: float32 [2048, 8192], P('ctx', 'wt')
- grad_w_down: float32 [8192, 2048], P('wt', 'ctx')
- grad_gain_post_ff: float32 [2048], P('ctx')
- grad_join_gate: float32 [2048, 256], P('ctx', 'wt')
- grad_join_proj: float32 [256, 2048], P('wt', 'ctx')
- grad_gain_join: float32 [2048], P('ctx')
Inputs may be any that keep to these rules, and one draw needn't show every extreme that they name: doc_lengths sum to 8192; the longest document has exactly 4096 tokens; documents may span several stretches. stretch_slots names every stretch of the stream once.
All inputs are finite; a program needn't handle non-finite values.
Results may differ from a plain program's by a relative error of at most 0.035.
Values may be sent and summed in bfloat16 or wider, within the bound.
No kernel may reach another device: no remote copies, remote signals or barrier semaphores. Data moves between devices by JAX's collectives and lax.ppermute only.
A program may use at most 192 MiB of HBM per device.

v0:
```python
import math

import jax
import jax.numpy as jnp
from jax import lax
from jax.sharding import PartitionSpec as P

epsilon = 1e-06
rope_base = 1000000.0
root_half = 0.7071067811865476
neg_big = -1e30
highest = lax.Precision.HIGHEST


def swapped(value, axis, bit):
    return lax.ppermute(value, axis, [(i, i ^ 1 << bit) for i in range(lax.axis_size(axis))])


def norm_gain(values, scales):
    return values * lax.rsqrt(jnp.mean(values * values, axis=-1, keepdims=True) + epsilon) * scales


def norm_plain(values):
    return values * lax.rsqrt(jnp.mean(values * values, axis=-1, keepdims=True) + epsilon)


def frequencies(head_dim):
    half_dim = head_dim // 2
    return 1.0 / rope_base ** (jnp.arange(half_dim, dtype=jnp.float32) * (2.0 / head_dim))


def rotate(values, cosine, sine_term):
    half_dim = values.shape[-1] // 2
    front_half = values[..., :half_dim]
    back_half = values[..., half_dim:]
    return jnp.concatenate(
        [front_half * cosine - back_half * sine_term, back_half * cosine + front_half * sine_term],
        axis=-1,
    )


def gelu_product(gate_pre, other_side):
    return jax.nn.gelu(gate_pre, approximate=True) * other_side


def product(left_side, right_side):
    return jnp.dot(left_side, right_side, preferred_element_type=jnp.float32)


def contract_rows(left_side, right_side):
    return lax.dot_general(
        left_side, right_side, (((0,), (0,)), ((), ())), preferred_element_type=jnp.float32
    )


def contract_cols(left_side, right_side):
    return lax.dot_general(
        left_side, right_side, (((1,), (1,)), ((), ())), preferred_element_type=jnp.float32
    )


def precise(left_side, right_side):
    return jnp.dot(
        left_side.astype(jnp.float32),
        right_side.astype(jnp.float32),
        precision=highest,
        preferred_element_type=jnp.float32,
    )


def precise_rows(left_side, right_side):
    return lax.dot_general(
        left_side.astype(jnp.float32),
        right_side,
        (((0,), (0,)), ((), ())),
        precision=highest,
        preferred_element_type=jnp.float32,
    )


def precise_cols(left_side, right_side):
    return lax.dot_general(
        left_side,
        right_side.astype(jnp.float32),
        (((1,), (1,)), ((), ())),
        precision=highest,
        preferred_element_type=jnp.float32,
    )


def lookup(indices, table):
    hits = indices[:, None] == jnp.arange(table.shape[0], dtype=jnp.int32)[None, :]
    return jnp.sum(jnp.where(hits, table[None, :], 0), axis=1)


def place_rows(row_ids, stretch_len, stretch_slots, doc_ends):
    positions = lookup(row_ids // stretch_len, stretch_slots) * stretch_len + row_ids % stretch_len
    segments = jnp.sum((doc_ends[None, :] <= positions[:, None]).astype(jnp.int32), axis=1)
    return (positions, segments)


def over_blocks(step_fn, running, pieces):
    length = pieces[0].shape[0]
    block_len = math.gcd(length, 1024)
    block_count = length // block_len

    def one_turn(block_no, state_now):
        block_parts = tuple(
            (
                lax.dynamic_slice_in_dim(source, block_no * block_len, block_len, 0)
                for source in pieces
            )
        )
        return step_fn(state_now, block_parts, block_no * block_len)

    return lax.fori_loop(0, block_count, one_turn, running)


def local(
    stream,
    layer_input,
    out_grad,
    doc_lengths,
    stretch_slots,
    gain_input,
    gain_query,
    gain_key,
    w_query,
    w_key,
    w_value,
    w_attn_out,
    gain_attn,
    laurel_left,
    laurel_right,
    gain_laurel,
    gain_pre_ff,
    w_gate,
    w_up,
    w_down,
    gain_post_ff,
    join_gate,
    join_proj,
    gain_join,
):
    row_count = stream.shape[0]
    stretch_len = row_count // 2
    head_dim = gain_query.shape[0]
    half_dim = head_dim // 2
    local_heads = w_query.shape[1] // head_dim
    score_scale = head_dim ** (-0.5)
    total_rows = row_count * lax.axis_size("ctx")
    doc_ends = jnp.cumsum(doc_lengths)
    row_ids = lax.axis_index("ctx") * row_count + jnp.arange(row_count, dtype=jnp.int32)
    positions, segments = place_rows(row_ids, stretch_len, stretch_slots, doc_ends)
    angles = positions.astype(jnp.float32)[:, None] * frequencies(head_dim)[None, :]
    cosine = jnp.cos(angles)
    sine_term = jnp.sin(angles)
    is_lower = lax.axis_index("wt") % 2 == 0
    stream_f = stream.astype(jnp.float32)
    normed, input_back = jax.vjp(norm_gain, stream_f, gain_input)
    normed_b = normed.astype(jnp.bfloat16)
    query_raw = product(normed_b, w_query)
    key_half = product(normed_b, w_key)
    value_half = product(normed_b, w_value)
    other_key, other_value = swapped((key_half, value_half), "wt", 0)
    key_full = jnp.where(
        is_lower,
        jnp.concatenate([key_half, other_key], axis=1),
        jnp.concatenate([other_key, key_half], axis=1),
    )
    value_full = jnp.where(
        is_lower,
        jnp.concatenate([value_half, other_value], axis=1),
        jnp.concatenate([other_value, value_half], axis=1),
    )

    def shape_query(raw_values, scales):
        per_head = raw_values.reshape(row_count, local_heads, head_dim)
        return rotate(norm_gain(per_head, scales), cosine[:, None, :], sine_term[:, None, :])

    def shape_key(raw_values, scales):
        return rotate(norm_gain(raw_values, scales), cosine, sine_term)

    query_rot, query_back = jax.vjp(shape_query, query_raw, gain_query)
    key_rot, key_back = jax.vjp(shape_key, key_full, gain_key)
    value_norm, value_back = jax.vjp(norm_plain, value_full)
    query_flat = (
        query_rot.astype(jnp.bfloat16).transpose(1, 0, 2).reshape(local_heads * row_count, head_dim)
    )
    key_b = key_rot.astype(jnp.bfloat16)
    value_b = value_norm.astype(jnp.bfloat16)
    query_pos = jnp.tile(positions, local_heads)
    query_seg = jnp.tile(segments, local_heads)
    flat_rows = local_heads * row_count

    def masked_scores(keys_blk, first_row):
        key_ids = first_row + jnp.arange(keys_blk.shape[0], dtype=jnp.int32)
        key_pos, key_seg = place_rows(key_ids, stretch_len, stretch_slots, doc_ends)
        allowed = (key_pos[None, :] <= query_pos[:, None]) & (
            key_seg[None, :] == query_seg[:, None]
        )
        scores = contract_cols(query_flat, keys_blk) * score_scale
        return (scores, allowed)

    def stats_step(running, pieces, first_row):
        row_max, row_total = running
        scores, allowed = masked_scores(pieces[0], first_row)
        scores = jnp.where(allowed, scores, neg_big)
        new_max = jnp.maximum(row_max, jnp.max(scores, axis=1))
        weights = jnp.where(allowed, jnp.exp(scores - new_max[:, None]), 0.0)
        row_total = row_total * jnp.exp(row_max - new_max) + jnp.sum(weights, axis=1)
        return (new_max, row_total)

    start_stats = (
        jnp.full((flat_rows,), neg_big, jnp.float32),
        jnp.zeros((flat_rows,), jnp.float32),
    )
    row_max, row_total = over_blocks(
        stats_step, start_stats, (lax.all_gather(key_b, "ctx", axis=0, tiled=True),)
    )
    log_total = row_max + jnp.log(row_total)

    def forward_step(running, pieces, first_row):
        accumulated, remainder = running
        keys_blk, values_blk = pieces
        scores, allowed = masked_scores(keys_blk, first_row)
        weights = jnp.where(allowed, jnp.exp(scores - log_total[:, None]), 0.0)
        weights_b = weights.astype(jnp.bfloat16)
        leftover = (weights - weights_b.astype(jnp.float32)).astype(jnp.bfloat16)
        accumulated = accumulated + product(weights_b, values_blk)
        remainder = remainder + product(leftover, values_blk)
        return (accumulated, remainder)

    start_forward = (
        jnp.zeros((flat_rows, head_dim), jnp.float32),
        jnp.zeros((flat_rows, head_dim), jnp.float32),
    )
    attn_flat, remainder = over_blocks(
        forward_step,
        start_forward,
        (
            lax.all_gather(key_b, "ctx", axis=0, tiled=True),
            lax.all_gather(value_b, "ctx", axis=0, tiled=True),
        ),
    )
    attn_exact = attn_flat + remainder
    attn_b = (
        attn_flat.reshape(local_heads, row_count, head_dim)
        .transpose(1, 0, 2)
        .reshape(row_count, local_heads * head_dim)
        .astype(jnp.bfloat16)
    )
    attn_part = product(attn_b, w_attn_out)
    laurel_mid = precise(normed_b, laurel_left)
    laurel_part = precise(laurel_mid, laurel_right)
    attn_sum, laurel_sum = lax.psum((attn_part, laurel_part), "wt")
    attn_normed, attn_nback = jax.vjp(norm_gain, attn_sum, gain_attn)
    laurel_normed, laurel_nback = jax.vjp(norm_gain, laurel_sum, gain_laurel)
    residual = (stream_f + attn_normed + normed + laurel_normed) * root_half
    pre_ff, pre_back = jax.vjp(norm_gain, residual, gain_pre_ff)
    pre_b = pre_ff.astype(jnp.bfloat16)
    gate_pre = product(pre_b, w_gate)
    up_pre = product(pre_b, w_up)
    activated, act_back = jax.vjp(gelu_product, gate_pre, up_pre)
    act_b = activated.astype(jnp.bfloat16)
    ff_part = product(act_b, w_down)
    ff_sum = lax.psum(ff_part, "wt")
    ff_normed, ff_nback = jax.vjp(norm_gain, ff_sum, gain_post_ff)
    after_ff = residual + ff_normed
    join_pre = precise(after_ff, join_gate)
    input_f = layer_input.astype(jnp.float32)
    joined, joined_back = jax.vjp(gelu_product, join_pre, input_f)
    join_part = precise(joined, join_proj)
    join_sum = lax.psum(join_part, "wt")
    join_normed, join_nback = jax.vjp(norm_gain, join_sum, gain_join)
    layer_out = after_ff + join_normed
    grad_top = out_grad.astype(jnp.float32)
    grad_join_sum, grad_gain_join = join_nback(grad_top)
    grad_join_proj = precise_rows(joined, grad_join_sum)
    grad_joined = precise_cols(grad_join_sum, join_proj)
    grad_join_pre, grad_input = joined_back(grad_joined)
    grad_join_gate = precise_rows(after_ff, grad_join_pre)
    grad_after = grad_top + lax.psum(precise_cols(grad_join_pre, join_gate), "wt")
    grad_ff_sum, grad_gain_post_ff = ff_nback(grad_after)
    grad_ff_b = grad_ff_sum.astype(jnp.bfloat16)
    grad_w_down = contract_rows(act_b, grad_ff_b)
    grad_activated = contract_cols(grad_ff_b, w_down)
    grad_gate, grad_upper = act_back(grad_activated)
    grad_gate_b = grad_gate.astype(jnp.bfloat16)
    grad_upper_b = grad_upper.astype(jnp.bfloat16)
    grad_w_gate = contract_rows(pre_b, grad_gate_b)
    grad_w_up = contract_rows(pre_b, grad_upper_b)
    pre_part = contract_cols(grad_gate_b, w_gate) + contract_cols(grad_upper_b, w_up)
    grad_pre = lax.psum(pre_part.astype(jnp.bfloat16), "wt").astype(jnp.float32)
    grad_resid_extra, grad_gain_pre_ff = pre_back(grad_pre)
    branch_grad = (grad_after + grad_resid_extra) * root_half
    grad_laurel_sum, grad_gain_laurel = laurel_nback(branch_grad)
    grad_laurel_right = precise_rows(laurel_mid, grad_laurel_sum)
    grad_mid = precise_cols(grad_laurel_sum, laurel_right)
    grad_laurel_left = precise_rows(normed_b, grad_mid)
    grad_attn_sum, grad_gain_attn = attn_nback(branch_grad)
    grad_attn_b = grad_attn_sum.astype(jnp.bfloat16)
    grad_w_attn_out = contract_rows(attn_b, grad_attn_b)
    grad_heads_rows = contract_cols(grad_attn_b, w_attn_out).astype(jnp.bfloat16)
    grad_heads = (
        grad_heads_rows.reshape(row_count, local_heads, head_dim)
        .transpose(1, 0, 2)
        .reshape(flat_rows, head_dim)
    )
    delta_rows = jnp.sum(grad_heads.astype(jnp.float32) * attn_exact, axis=1)

    def backward_step(running, pieces, first_row):
        grad_query, grad_keys, grad_values = running
        keys_blk, values_blk = pieces
        block_rows = keys_blk.shape[0]
        scores, allowed = masked_scores(keys_blk, first_row)
        weights = jnp.where(allowed, jnp.exp(scores - log_total[:, None]), 0.0)
        grad_weights = contract_cols(grad_heads, values_blk)
        grad_scores = (weights * (grad_weights - delta_rows[:, None])).astype(jnp.bfloat16)
        grad_query = grad_query + product(grad_scores, keys_blk) * score_scale
        key_term = contract_rows(grad_scores, query_flat) * score_scale
        value_term = contract_rows(weights.astype(jnp.bfloat16), grad_heads)
        old_keys = lax.dynamic_slice_in_dim(grad_keys, first_row, block_rows, 0)
        grad_keys = lax.dynamic_update_slice_in_dim(grad_keys, old_keys + key_term, first_row, 0)
        old_values = lax.dynamic_slice_in_dim(grad_values, first_row, block_rows, 0)
        grad_values = lax.dynamic_update_slice_in_dim(
            grad_values, old_values + value_term, first_row, 0
        )
        return (grad_query, grad_keys, grad_values)

    start_backward = (
        jnp.zeros((flat_rows, head_dim), jnp.float32),
        jnp.zeros((total_rows, head_dim), jnp.float32),
        jnp.zeros((total_rows, head_dim), jnp.float32),
    )
    grad_query_flat, grad_keys_all, grad_values_all = over_blocks(
        backward_step,
        start_backward,
        (
            lax.all_gather(key_b, "ctx", axis=0, tiled=True),
            lax.all_gather(value_b, "ctx", axis=0, tiled=True),
        ),
    )
    grad_key_rows, grad_value_rows = (
        lax.psum_scatter(
            grad_keys_all.astype(jnp.bfloat16), "ctx", scatter_dimension=0, tiled=True
        ).astype(jnp.float32),
        lax.psum_scatter(
            grad_values_all.astype(jnp.bfloat16), "ctx", scatter_dimension=0, tiled=True
        ).astype(jnp.float32),
    )
    grad_query_rot = grad_query_flat.reshape(local_heads, row_count, head_dim).transpose(1, 0, 2)
    grad_query_raw, grad_gain_query_part = query_back(grad_query_rot)
    grad_key_full, grad_gain_key_part = key_back(grad_key_rows)
    (grad_value_full,) = value_back(grad_value_rows)
    key_front = grad_key_full[:, :half_dim]
    key_rear = grad_key_full[:, half_dim:]
    value_front = grad_value_full[:, :half_dim]
    value_rear = grad_value_full[:, half_dim:]
    sent_key = jnp.where(is_lower, key_rear, key_front)
    sent_value = jnp.where(is_lower, value_rear, value_front)
    recv_key, recv_value = (
        swapped(sent_key.astype(jnp.bfloat16), "wt", 0).astype(sent_key.dtype),
        swapped(sent_value.astype(jnp.bfloat16), "wt", 0).astype(sent_value.dtype),
    )
    grad_key_b = (jnp.where(is_lower, key_front, key_rear) + recv_key).astype(jnp.bfloat16)
    grad_value_b = (jnp.where(is_lower, value_front, value_rear) + recv_value).astype(jnp.bfloat16)
    grad_query_b = grad_query_raw.astype(jnp.bfloat16)
    grad_w_query = contract_rows(normed_b, grad_query_b)
    grad_w_key = contract_rows(normed_b, grad_key_b)
    grad_w_value = contract_rows(normed_b, grad_value_b)
    normed_part = (
        contract_cols(grad_query_b, w_query)
        + contract_cols(grad_key_b, w_key)
        + contract_cols(grad_value_b, w_value)
        + precise_cols(grad_mid, laurel_left)
    )
    normed_sum, grad_gain_query, grad_gain_key = (
        lax.psum(normed_part.astype(jnp.bfloat16), "wt").astype(jnp.float32),
        lax.psum(grad_gain_query_part.astype(jnp.bfloat16), "wt").astype(jnp.float32),
        lax.psum(grad_gain_key_part.astype(jnp.bfloat16), "wt").astype(jnp.float32),
    )
    grad_stream_extra, grad_gain_input = input_back(branch_grad + normed_sum)
    stream_grad = branch_grad + grad_stream_extra
    rows_out = (
        lax.psum_scatter(
            grad_w_query.astype(jnp.bfloat16), "ctx", scatter_dimension=0, tiled=True
        ).astype(jnp.float32),
        lax.psum_scatter(
            grad_w_key.astype(jnp.bfloat16), "ctx", scatter_dimension=0, tiled=True
        ).astype(jnp.float32),
        lax.psum_scatter(
            grad_w_value.astype(jnp.bfloat16), "ctx", scatter_dimension=0, tiled=True
        ).astype(jnp.float32),
        lax.psum_scatter(
            grad_laurel_left.astype(jnp.bfloat16), "ctx", scatter_dimension=0, tiled=True
        ).astype(jnp.float32),
        lax.psum_scatter(
            grad_w_gate.astype(jnp.bfloat16), "ctx", scatter_dimension=0, tiled=True
        ).astype(jnp.float32),
        lax.psum_scatter(
            grad_w_up.astype(jnp.bfloat16), "ctx", scatter_dimension=0, tiled=True
        ).astype(jnp.float32),
        lax.psum_scatter(
            grad_join_gate.astype(jnp.bfloat16), "ctx", scatter_dimension=0, tiled=True
        ).astype(jnp.float32),
    )
    gain_stack = jnp.stack(
        [
            grad_gain_input,
            grad_gain_attn,
            grad_gain_laurel,
            grad_gain_pre_ff,
            grad_gain_post_ff,
            grad_gain_join,
        ],
        axis=0,
    )
    head_stack = jnp.stack([grad_gain_query, grad_gain_key], axis=0)
    cols_out = (
        lax.psum_scatter(
            grad_w_attn_out.astype(jnp.bfloat16), "ctx", scatter_dimension=1, tiled=True
        ).astype(jnp.float32),
        lax.psum_scatter(
            grad_laurel_right.astype(jnp.bfloat16), "ctx", scatter_dimension=1, tiled=True
        ).astype(jnp.float32),
        lax.psum_scatter(
            grad_w_down.astype(jnp.bfloat16), "ctx", scatter_dimension=1, tiled=True
        ).astype(jnp.float32),
        lax.psum_scatter(
            grad_join_proj.astype(jnp.bfloat16), "ctx", scatter_dimension=1, tiled=True
        ).astype(jnp.float32),
        lax.psum_scatter(
            gain_stack.astype(jnp.bfloat16), "ctx", scatter_dimension=1, tiled=True
        ).astype(jnp.float32),
        lax.psum_scatter(
            head_stack.astype(jnp.bfloat16), "ctx", scatter_dimension=1, tiled=True
        ).astype(jnp.float32),
    )
    gains_part = cols_out[4]
    heads_part = cols_out[5]
    return (
        layer_out,
        stream_grad,
        grad_input,
        gains_part[0],
        heads_part[0],
        heads_part[1],
        rows_out[0],
        rows_out[1],
        rows_out[2],
        cols_out[0],
        gains_part[1],
        rows_out[3],
        cols_out[1],
        gains_part[2],
        gains_part[3],
        rows_out[4],
        rows_out[5],
        cols_out[2],
        gains_part[4],
        rows_out[6],
        cols_out[3],
        gains_part[5],
    )


def solution(mesh):
    return jax.shard_map(
        local,
        mesh=mesh,
        in_specs=(
            P("ctx", None),
            P("ctx", "wt"),
            P("ctx", None),
            P(),
            P(),
            P(),
            P(),
            P(),
            P(None, "wt"),
            P(None, "wt"),
            P(None, "wt"),
            P("wt", None),
            P(),
            P(None, "wt"),
            P("wt", None),
            P(),
            P(),
            P(None, "wt"),
            P(None, "wt"),
            P("wt", None),
            P(),
            P(None, "wt"),
            P("wt", None),
            P(),
        ),
        out_specs=(
            P("ctx", None),
            P("ctx", None),
            P("ctx", "wt"),
            P("ctx"),
            P("ctx"),
            P("ctx"),
            P("ctx", "wt"),
            P("ctx", "wt"),
            P("ctx", "wt"),
            P("wt", "ctx"),
            P("ctx"),
            P("ctx", "wt"),
            P("wt", "ctx"),
            P("ctx"),
            P("ctx"),
            P("ctx", "wt"),
            P("ctx", "wt"),
            P("wt", "ctx"),
            P("ctx"),
            P("ctx", "wt"),
            P("wt", "ctx"),
            P("ctx"),
        ),
        check_vma=False,
    )
```

profile of v0, /device:TPU:1, one launch (start us, length us, event | category | flops | bytes accessed | tf_op | source)
XLA Modules:
  0.0 3465.2 jit_solution(3658251190622853694)
XLA Ops:
  20.1 3.1 fusion.127
  36.9 75.9 %all-gather.3.cloned.1.call-done = bf16[8192,256]{0,1:T(8,128)(2,1)} async-done(((bf16[256,256]{0,1:T(8,128)(2,1)}), bf16[8192,256]{0,1:T(8,128)(2,1)}) %all-gather.3.cloned.1.call-update) | async-done | bytes 4194320 | tf_op jit(solution)/shard_map/all_gather | solution.py:242
  112.8 6.4 copy.130
  119.2 29.9 while.56
  149.2 58.6 %all-gather.5.cloned.1.call-done = bf16[8192,256]{0,1:T(8,128)(2,1)} async-done(((bf16[256,256]{0,1:T(8,128)(2,1)}), bf16[8192,256]{0,1:T(8,128)(2,1)}) %all-gather.5.cloned.1.call-update) | async-done | bytes 4194320 | tf_op jit(solution)/shard_map/all_gather | solution.py:243
  207.8 6.4 copy.131
  214.1 49.8 %while.57 = (s32[]{:T(128)}, f32[512,256]{1,0:T(8,128)S(1)}, f32[512,256]{1,0:T(8,128)S(1)}, s32[64]{0:T(128)S(1)}, s32[8]{0:T(128)}, /*index=5*/bf16[8192,256]{...) while((s32[]{:T(128)}, f32[512,256]{1,0:T(8,128)S(1)}, ...), condition=%wide.region_16.17_spmd.clone, body=%wide.region_13.16_spmd.clone.sunk | while | flops 811847680 | bytes 10281474 | solution.py:116
  266.6 3.0 fusion.129
  269.9 89.8 %all-reduce.24.cloned.1.call-done = (f32[256,2048]{1,0:T(8,128)}, f32[256,2048]{1,0:T(8,128)}) async-done(((f32[256,2048]{1,0:T(8,128)}, f32[256,2048]{1,0:T(8,128)}), (f32[256,2048]{1,0:T(8,128)}, f32[256,2048]{1,0:T(8,128)})) %all-reduce.24.cloned.1.call-update) | async-done | bytes 4194320 | tf_op jit(solution)/shard_map/psum | solution.py:256
  359.7 2.7 multiply_reduce_fusion.9
  365.9 6.3 fusion.132
  373.1 4.0 multiply_convert_fusion.1
  378.1 3.7 fusion.133
  381.9 58.5 %all-reduce.14.cloned.1.call-done = f32[256,2048]{1,0:T(8,128)} async-done(((f32[256,2048]{1,0:T(8,128)}), f32[256,2048]{1,0:T(8,128)}) %all-reduce.14.cloned.1.call-update) | async-done | bytes 2097168 | tf_op jit(solution)/shard_map/psum | solution.py:267
  450.0 58.4 %all-reduce.16.cloned.1.call-done = f32[256,2048]{1,0:T(8,128)} async-done(((f32[256,2048]{1,0:T(8,128)}), f32[256,2048]{1,0:T(8,128)}) %all-reduce.16.cloned.1.call-update) | async-done | bytes 2097168 | tf_op jit(solution)/shard_map/psum | solution.py:274
  510.6 4.6 fusion.76
  517.5 2.5 fusion.120
  520.1 58.6 %all-reduce.18.cloned.1.call-done = f32[256,2048]{1,0:T(8,128)} async-done(((f32[256,2048]{1,0:T(8,128)}), f32[256,2048]{1,0:T(8,128)}) %all-reduce.18.cloned.1.call-update) | async-done | bytes 2097168 | tf_op jit(solution)/shard_map/psum | solution.py:283
  578.8 3.6 multiply_reduce_fusion
  584.0 8.3 multiply_convert_fusion
  592.4 2.4 fusion.135
  594.8 6.7 fusion.54
  602.1 42.2 %all-reduce.20.cloned.1.call-done = bf16[256,2048]{1,0:T(8,128)(2,1)} async-done(((bf16[256,2048]{1,0:T(8,128)(2,1)}), bf16[256,2048]{1,0:T(8,128)(2,1)}) %all-reduce.20.cloned.1.call-update) | async-done | bytes 1048592 | tf_op jit(solution)/shard_map/psum | solution.py:294
  644.3 3.4 fusion.68
  647.8 5.1 multiply_reduce_fusion.1
  658.1 4.3 broadcast.1080.clone2
  662.4 4.3 broadcast.1080.clone
  666.7 132.2 %while.58 = (s32[]{:T(128)}, f32[512,256]{1,0:T(8,128)}, f32[8192,256]{0,1:T(8,128)}, f32[8192,256]{0,1:T(8,128)}, s32[64]{0:T(128)S(1)}, /*index=5*/s32[8]{0:T(...) while((s32[]{:T(128)}, f32[512,256]{1,0:T(8,128)}, ...), condition=%wide.region_36.37_spmd.clone, body=%wide.region_33.36_spmd.clone.sunk | while | flops 1348849664 | bytes 39389816 | solution.py:116
  678.5 2.4 fusion.253
  694.9 2.6 fusion.253
  711.4 2.6 fusion.253
  728.0 2.6 fusion.253
  744.5 2.6 fusion.253
  761.1 2.6 fusion.253
  777.6 2.6 fusion.253
  794.2 2.6 fusion.253
  798.9 5.9 convert_element_type.311
  804.9 6.0 convert_element_type.306
  819.6 155.8 %reduce-scatter.26.cloned.1.call-done = bf16[256,256]{0,1:T(8,128)(2,1)} async-done(((bf16[8192,256]{0,1:T(8,128)(2,1)}), bf16[256,256]{0,1:T(8,128)(2,1)}) %reduce-scatter.26.cloned.1.call-update) | async-done | bytes 131088 | tf_op jit(solution)/shard_map/reduce_scatter | solution.py:348
  977.1 187.8 %reduce-scatter.24.cloned.1.call-done = bf16[256,256]{0,1:T(8,128)(2,1)} async-done(((bf16[8192,256]{0,1:T(8,128)(2,1)}), bf16[256,256]{0,1:T(8,128)(2,1)}) %reduce-scatter.24.cloned.1.call-update) | async-done | bytes 131088 | tf_op jit(solution)/shard_map/reduce_scatter | solution.py:345
  1170.0 23.7 collective-permute-start.2
  1198.2 3.4 convolution_convert_fusion.8
  1202.9 5.9 convolution_convert_fusion.5
  1210.5 2.7 convolution_convert_fusion.9
  1222.4 12.2 all-reduce.22.cloned.1.call-done
  1234.6 2.9 fusion.65
  1238.7 5.7 convolution_convert_fusion
  1246.0 5.7 convolution_convert_fusion.1
  1252.9 5.7 convolution_convert_fusion.2
  1260.5 135.5 %reduce-scatter.50.cloned.1.call-done = bf16[64,64]{1,0:T(8,128)(2,1)} async-done(((bf16[2048,64]{1,0:T(8,128)(2,1)}), bf16[64,64]{1,0:T(8,128)(2,1)}) %reduce-scatter.50.cloned.1.call-update) | async-done | bytes 8208
  1397.5 180.2 %reduce-scatter.42.cloned.1.call-done = bf16[64,64]{1,0:T(8,128)(2,1)} async-done(((bf16[2048,64]{1,0:T(8,128)(2,1)}), bf16[64,64]{1,0:T(8,128)(2,1)}) %reduce-scatter.42.cloned.1.call-update) | async-done | bytes 8208 | tf_op jit(solution)/shard_map/reduce_scatter | solution.py:404
  1579.0 179.7 %reduce-scatter.46.cloned.1.call-done = bf16[64,16]{1,0:T(8,128)(2,1)} async-done(((bf16[2048,16]{1,0:T(8,128)(2,1)}), bf16[64,16]{1,0:T(8,128)(2,1)}) %reduce-scatter.46.cloned.1.call-update) | async-done | bytes 2064
  1760.1 179.9 %reduce-scatter.48.cloned.1.call-done = bf16[64,16]{1,0:T(8,128)(2,1)} async-done(((bf16[2048,16]{1,0:T(8,128)(2,1)}), bf16[64,16]{1,0:T(8,128)(2,1)}) %reduce-scatter.48.cloned.1.call-update) | async-done | bytes 2064
  1941.3 184.4 %reduce-scatter.34.cloned.1.call-done = bf16[512,64]{0,1:T(8,128)(2,1)} async-done(((bf16[512,2048]{0,1:T(8,128)(2,1)}), bf16[512,64]{0,1:T(8,128)(2,1)}) %reduce-scatter.34.cloned.1.call-update) | async-done | bytes 65552 | tf_op jit(solution)/shard_map/reduce_scatter | solution.py:421
  2127.2 183.1 %reduce-scatter.28.cloned.1.call-done = bf16[64,512]{1,0:T(8,128)(2,1)} async-done(((bf16[2048,512]{1,0:T(8,128)(2,1)}), bf16[64,512]{1,0:T(8,128)(2,1)}) %reduce-scatter.28.cloned.1.call-update) | async-done | bytes 65552 | tf_op jit(solution)/shard_map/reduce_scatter | solution.py:386
  2311.9 30.2 all-reduce.6
  2342.0 77.1 %all-reduce.4 = bf16[2,256]{1,0:T(2,128)(2,1)S(1)} all-reduce(bf16[2,256]{1,0:T(2,128)(2,1)S(1)} %pad_maximum_fusion.1), channel_id=5, replica_groups=mesh['ctx'=32,'wt'=4] {'ctx'}, use_global_device_ids=true, to_apply=%region_56.57.clone | all-reduce | flops 512 | bytes 2048
  2419.7 71.4 %reduce-scatter.32.cloned.1.call-done = bf16[64,128]{1,0:T(8,128)(2,1)} async-done(((bf16[2048,128]{1,0:T(8,128)(2,1)}), bf16[64,128]{1,0:T(8,128)(2,1)}) %reduce-scatter.32.cloned.1.call-update) | async-done | bytes 16400 | tf_op jit(solution)/shard_map/reduce_scatter | solution.py:392
  2492.5 180.3 %reduce-scatter.30.cloned.1.call-done = bf16[64,128]{1,0:T(8,128)(2,1)} async-done(((bf16[2048,128]{1,0:T(8,128)(2,1)}), bf16[64,128]{1,0:T(8,128)(2,1)}) %reduce-scatter.30.cloned.1.call-update) | async-done | bytes 16400 | tf_op jit(solution)/shard_map/reduce_scatter | solution.py:389
  2674.1 4.4 fusion.80
  2678.5 176.4 %reduce-scatter.44.cloned.1.call-done = bf16[64,6]{1,0:T(8,128)(2,1)} async-done(((bf16[2048,6]{1,0:T(8,128)(2,1)}), bf16[64,6]{1,0:T(8,128)(2,1)}) %reduce-scatter.44.cloned.1.call-update) | async-done | bytes 784
  2856.3 200.4 %reduce-scatter.40.cloned.1.call-done = bf16[2048,64]{0,1:T(8,128)(2,1)} async-done(((bf16[2048,2048]{0,1:T(8,128)(2,1)}), bf16[2048,64]{0,1:T(8,128)(2,1)}) %reduce-scatter.40.cloned.1.call-update) | async-done | bytes 262160 | tf_op jit(solution)/shard_map/reduce_scatter | solution.py:427
  3058.4 199.4 %reduce-scatter.38.cloned.1.call-done = bf16[64,2048]{1,0:T(8,128)(2,1)} async-done(((bf16[2048,2048]{1,0:T(8,128)(2,1)}), bf16[64,2048]{1,0:T(8,128)(2,1)}) %reduce-scatter.38.cloned.1.call-update) | async-done | bytes 262160 | tf_op jit(solution)/shard_map/reduce_scatter | solution.py:401
  3259.6 196.5 %reduce-scatter.36.cloned.1.call-done = bf16[64,2048]{1,0:T(8,128)(2,1)} async-done(((bf16[2048,2048]{1,0:T(8,128)(2,1)}), bf16[64,2048]{1,0:T(8,128)(2,1)}) %reduce-scatter.36.cloned.1.call-update) | async-done | bytes 262160 | tf_op jit(solution)/shard_map/reduce_scatter | solution.py:398
  (856 shorter events, 300.3 us)
Async XLA Ops:
  7.2 259.4 %copy-start = (bf16[512,2048]{1,0:T(8,128)(2,1)S(1)}, bf16[512,2048]{1,0:T(8,128)(2,1)}, u32[]{:S(2)}) copy-start(bf16[512,2048]{1,0:T(8,128)(2,1)} %param.41) | copy-start | bytes 6291460
  7.2 105.6 %all-gather.3.cloned.1.call-start = ((), (), s32[]{:S(2)}) async-start(), calls=%async_computation.14 | async-start | bytes 4325376 | tf_op jit(solution)/shard_map/all_gather | solution.py:242
  11.1 17.1 copy-start.3
  11.6 2.5 collective-permute-start
  16.7 191.1 %all-gather.5.cloned.1.call-start = ((), (), s32[]{:S(2)}) async-start(), calls=%async_computation.15 | async-start | bytes 4325376 | tf_op jit(solution)/shard_map/all_gather | solution.py:243
  18.3 16.8 copy-start.41
  18.3 15.8 collective-permute-start.1
  33.3 85.9 %copy-start.54 = (f32[256,128]{1,0:T(8,128)}, f32[256,128]{1,0:T(8,128)S(1)}, u32[]{:S(2)}) copy-start(f32[256,128]{1,0:T(8,128)S(1)} %copy.126) | copy-start | bytes 393220
  33.4 85.8 %copy-start.56 = (f32[256,128]{1,0:T(8,128)}, f32[256,128]{1,0:T(8,128)S(1)}, u32[]{:S(2)}) copy-start(f32[256,128]{1,0:T(8,128)S(1)} %copy.127) | copy-start | bytes 393220
  35.1 84.1 %copy-start.125 = (f32[256]{0:T(256)}, f32[256]{0:T(256)S(1)}, u32[]{:S(2)}) copy-start(f32[256]{0:T(256)S(1)} %multiply_reduce_fusion.17) | copy-start | bytes 3076
  35.1 84.1 %copy-start.121 = (f32[256]{0:T(256)}, f32[256]{0:T(256)S(1)}, u32[]{:S(2)}) copy-start(f32[256]{0:T(256)S(1)} %fusion.111) | copy-start | bytes 3076
  36.8 82.4 %copy-start.91 = (f32[512]{0:T(512)S(1)}, f32[512]{0:T(512)}, u32[]{:S(2)}) copy-start(f32[512]{0:T(512)} %custom-call.1) | copy-start | bytes 6148
  36.9 322.8 %all-reduce.24.cloned.1.call-start = ((), (), s32[]{:S(2)}) async-start(), calls=%async_computation.35 | async-start | bytes 8388608 | tf_op jit(solution)/shard_map/psum | solution.py:256
  149.1 65.0 %copy-start.20 = (f32[512,256]{1,0:T(8,128)S(1)}, f32[512,256]{1,0:T(8,128)}, u32[]{:S(2)}) copy-start(f32[512,256]{1,0:T(8,128)} %custom-call.2) | copy-start | bytes 1572868
  149.2 65.0 %copy-start.25 = (f32[512,256]{1,0:T(8,128)S(1)}, f32[512,256]{1,0:T(8,128)}, u32[]{:S(2)}) copy-start(f32[512,256]{1,0:T(8,128)} %custom-call.3) | copy-start | bytes 1572868
  269.6 93.4 %copy-start.18 = (bf16[256,2048]{1,0:T(8,128)(2,1)S(1)}, bf16[256,2048]{1,0:T(8,128)(2,1)}, u32[]{:S(2)}) copy-start(bf16[256,2048]{1,0:T(8,128)(2,1)} %param.30) | copy-start | bytes 3145732
  269.6 93.4 %copy-start.92 = (f32[2048]{0:T(1024)S(1)}, f32[2048]{0:T(1024)}, u32[]{:S(2)}) copy-start(f32[2048]{0:T(1024)} %param.45) | copy-start | bytes 24580
  269.7 93.4 %copy-start.94 = (f32[2048]{0:T(1024)S(1)}, f32[2048]{0:T(1024)}, u32[]{:S(2)}) copy-start(f32[2048]{0:T(1024)} %param.42) | copy-start | bytes 24580
  269.7 170.7 %all-reduce.14.cloned.1.call-start = ((), (), s32[]{:S(2)}) async-start(), calls=%async_computation.16 | async-start | bytes 4194304 | tf_op jit(solution)/shard_map/psum | solution.py:267
  381.8 60.6 %copy-start.83 = (f32[2048]{0:T(1024)S(1)}, f32[2048]{0:T(1024)}, u32[]{:S(2)}) copy-start(f32[2048]{0:T(1024)} %param.50) | copy-start | bytes 24580
  381.8 126.6 %all-reduce.16.cloned.1.call-start = ((), (), s32[]{:S(2)}) async-start(), calls=%async_computation.17 | async-start | bytes 4194304 | tf_op jit(solution)/shard_map/psum | solution.py:274
  449.7 60.7 %copy-start.8 = (bf16[256,2048]{1,0:T(8,128)(2,1)S(1)}, bf16[256,2048]{1,0:T(8,128)(2,1)}, u32[]{:S(2)}) copy-start(bf16[256,2048]{1,0:T(8,128)(2,1)} %param.32) | copy-start | bytes 3145732
  449.7 60.7 %copy-start.87 = (f32[2048]{0:T(1024)S(1)}, f32[2048]{0:T(1024)}, u32[]{:S(2)}) copy-start(f32[2048]{0:T(1024)} %param.53) | copy-start | bytes 24580
  449.8 129.0 %all-reduce.18.cloned.1.call-start = ((), (), s32[]{:S(2)}) async-start(), calls=%async_computation.18 | async-start | bytes 4194304 | tf_op jit(solution)/shard_map/psum | solution.py:283
  517.5 61.2 %copy-start.84 = (f32[2048]{0:T(1024)S(1)}, f32[2048]{0:T(1024)}, u32[]{:S(2)}) copy-start(f32[2048]{0:T(1024)} %param.50) | copy-start | bytes 24580
  517.5 61.2 %copy-start.114 = (f32[256]{0:T(256)S(1)}, f32[256]{0:T(256)}, u32[]{:S(2)}) copy-start(f32[256]{0:T(256)} %copy-done.113) | copy-start | bytes 3076
  520.1 62.3 %copy-start.128 = (f32[256]{0:T(256)S(1)}, f32[256]{0:T(256)}, u32[]{:S(2)}) copy-start(f32[256]{0:T(256)} %copy-done.127) | copy-start | bytes 3076
  520.1 124.2 %all-reduce.20.cloned.1.call-start = ((), (), s32[]{:S(2)}) async-start(), calls=%async_computation.19 | async-start | bytes 2097152 | tf_op jit(solution)/shard_map/psum | solution.py:294
  594.8 49.5 %copy-start.86 = (f32[2048]{0:T(1024)S(1)}, f32[2048]{0:T(1024)}, u32[]{:S(2)}) copy-start(f32[2048]{0:T(1024)} %param.46) | copy-start | bytes 24580
  594.8 49.5 %copy-start.120 = (f32[256]{0:T(256)S(1)}, f32[256]{0:T(256)}, u32[]{:S(2)}) copy-start(f32[256]{0:T(256)} %copy-done.119) | copy-start | bytes 3076
  601.5 46.2 %copy-start.135 = (f32[256]{0:T(256)S(1)}, f32[256]{0:T(256)}, u32[]{:S(2)}) copy-start(f32[256]{0:T(256)} %copy-done.134) | copy-start | bytes 3076
  601.5 46.2 %copy-start.110 = (f32[256]{0:T(256)S(1)}, f32[256]{0:T(256)}, u32[]{:S(2)}) copy-start(f32[256]{0:T(256)} %copy-done.109) | copy-start | bytes 3076
  601.5 46.2 %copy-start.112 = (f32[256]{0:T(256)S(1)}, f32[256]{0:T(256)}, u32[]{:S(2)}) copy-start(f32[256]{0:T(256)} %copy-done.111) | copy-start | bytes 3076
  601.5 46.2 %copy-start.136 = (f32[256]{0:T(256)S(1)}, f32[256]{0:T(256)}, u32[]{:S(2)}) copy-start(f32[256]{0:T(256)} %get-tuple-element.1351) | copy-start | bytes 3076
  601.6 373.8 %reduce-scatter.26.cloned.1.call-start = ((), (), s32[]{:S(2)}) async-start(), calls=%async_computation.21 | async-start | bytes 4325376 | tf_op jit(solution)/shard_map/reduce_scatter | solution.py:348
  804.9 360.0 %reduce-scatter.24.cloned.1.call-start = ((), (), s32[]{:S(2)}) async-start(), calls=%async_computation.20 | async-start | bytes 4325376 | tf_op jit(solution)/shard_map/reduce_scatter | solution.py:345
  811.1 423.5 %all-reduce.22.cloned.1.call-start = ((), (), s32[]{:S(2)}) async-start(), calls=%async_computation.22 | async-start | bytes 2097152 | tf_op jit(solution)/shard_map/psum | solution.py:379
  818.8 156.6 %copy-start.42 = (f32[256,128]{0,1:T(8,128)S(1)}, f32[256,128]{0,1:T(8,128)}, u32[]{:S(2)}) copy-start(f32[256,128]{0,1:T(8,128)} %copy-done.41) | copy-start | bytes 393220
  818.9 157.6 %copy-start.126 = (f32[256]{0:T(256)S(1)}, f32[256]{0:T(256)}, u32[]{:S(2)}) copy-start(f32[256]{0:T(256)} %copy-done.125) | copy-start | bytes 3076
  818.9 348.2 %copy-start.40 = (f32[256,128]{0,1:T(8,128)S(1)}, f32[256,128]{0,1:T(8,128)}, u32[]{:S(2)}) copy-start(f32[256,128]{0,1:T(8,128)} %copy-done.39) | copy-start | bytes 393220
  818.9 348.2 %copy-start.49 = (f32[256,128]{0,1:T(8,128)S(1)}, f32[256,128]{0,1:T(8,128)}, u32[]{:S(2)}) copy-start(f32[256,128]{0,1:T(8,128)} %copy-done.48) | copy-start | bytes 393220
  819.6 375.2 %copy-start.45 = (bf16[2048,128]{1,0:T(8,128)(2,1)S(1)}, bf16[2048,128]{1,0:T(8,128)(2,1)}, u32[]{:S(2)}) copy-start(bf16[2048,128]{1,0:T(8,128)(2,1)} %param.39) | copy-start | bytes 1572868
  1164.8 28.8 copy-start.72
  1164.8 28.8 copy-start.137
  1170.0 24.9 collective-permute-start.2
  1194.7 1.3 collective-permute-start.3
  1198.1 197.9 %reduce-scatter.50.cloned.1.call-start = ((), (), s32[]{:S(2)}) async-start(), calls=%async_computation.34 | async-start | bytes 540672
  1202.7 374.9 %reduce-scatter.42.cloned.1.call-start = ((), (), s32[]{:S(2)}) async-start(), calls=%async_computation.30 | async-start | bytes 540672 | tf_op jit(solution)/shard_map/reduce_scatter | solution.py:404
  1208.8 549.8 %reduce-scatter.46.cloned.1.call-start = ((), (), s32[]{:S(2)}) async-start(), calls=%async_computation.32 | async-start | bytes 540672
  1210.5 729.5 %reduce-scatter.48.cloned.1.call-start = ((), (), s32[]{:S(2)}) async-start(), calls=%async_computation.33 | async-start | bytes 540672
  1214.3 911.4 %reduce-scatter.34.cloned.1.call-start = ((), (), s32[]{:S(2)}) async-start(), calls=%async_computation.26 | async-start | bytes 2162688 | tf_op jit(solution)/shard_map/reduce_scatter | solution.py:421
  1216.6 1093.8 %reduce-scatter.28.cloned.1.call-start = ((), (), s32[]{:S(2)}) async-start(), calls=%async_computation.23 | async-start | bytes 2162688 | tf_op jit(solution)/shard_map/reduce_scatter | solution.py:386
  1218.8 1272.3 %reduce-scatter.32.cloned.1.call-start = ((), (), s32[]{:S(2)}) async-start(), calls=%async_computation.25 | async-start | bytes 540672 | tf_op jit(solution)/shard_map/reduce_scatter | solution.py:392
  1220.8 1451.9 %reduce-scatter.30.cloned.1.call-start = ((), (), s32[]{:S(2)}) async-start(), calls=%async_computation.24 | async-start | bytes 540672 | tf_op jit(solution)/shard_map/reduce_scatter | solution.py:389
  1222.2 1632.7 %reduce-scatter.44.cloned.1.call-start = ((), (), s32[]{:S(2)}) async-start(), calls=%async_computation.31 | async-start | bytes 540672
  1222.4 16.3 copy-start.36
  1222.4 16.3 copy-start.53
  1238.6 1818.0 %reduce-scatter.40.cloned.1.call-start = ((), (), s32[]{:S(2)}) async-start(), calls=%async_computation.29 | async-start | bytes 8650752 | tf_op jit(solution)/shard_map/reduce_scatter | solution.py:427
  1244.5 2013.4 %reduce-scatter.38.cloned.1.call-start = ((), (), s32[]{:S(2)}) async-start(), calls=%async_computation.28 | async-start | bytes 8650752 | tf_op jit(solution)/shard_map/reduce_scatter | solution.py:401
  1251.7 2204.5 %reduce-scatter.36.cloned.1.call-start = ((), (), s32[]{:S(2)}) async-start(), calls=%async_computation.27 | async-start | bytes 8650752 | tf_op jit(solution)/shard_map/reduce_scatter | solution.py:398
  1258.6 320.3 %copy-start.140 = (bf16[256]{0:T(256)(128)(2,1)S(1)}, bf16[256]{0:T(256)(128)(2,1)}, u32[]{:S(2)}) copy-start(bf16[256]{0:T(256)(128)(2,1)} %get-tuple-element.1237) | copy-start | bytes 1540
  1258.6 1053.2 %copy-start.141 = (bf16[256]{0:T(256)(128)(2,1)S(1)}, bf16[256]{0:T(256)(128)(2,1)}, u32[]{:S(2)}) copy-start(bf16[256]{0:T(256)(128)(2,1)} %get-tuple-element.1239) | copy-start | bytes 1540
  1258.6 1415.5 %copy-start.123 = (f32[256]{0:T(256)S(1)}, f32[256]{0:T(256)}, u32[]{:S(2)}) copy-start(f32[256]{0:T(256)} %copy-done.122) | copy-start | bytes 3076
  2674.1 783.8 %copy-start.1 = (bf16[512,2048]{1,0:T(8,128)(2,1)S(1)}, bf16[512,2048]{1,0:T(8,128)(2,1)}, u32[]{:S(2)}) copy-start(bf16[512,2048]{1,0:T(8,128)(2,1)} %param.41) | copy-start | bytes 6291460
  (134 other events, 481.8 us)
Sparse Core Ops, SparseCore 0:
  16.8 95.9 all-gather.2
  116.2 91.5 all-gather.4
  269.8 89.8 all-reduce.23
  382.0 58.4 all-reduce.13
  449.9 58.4 all-reduce.15
  520.2 58.5 all-reduce.17
  601.7 42.5 all-reduce.19
  805.0 170.3 reduce-scatter.25
  977.9 186.8 reduce-scatter.23
  1198.2 36.3 all-reduce.21
  1237.0 159.0 reduce-scatter.49
  1398.3 179.2 reduce-scatter.41
  1580.0 178.6 reduce-scatter.45
  1761.0 178.9 reduce-scatter.47
  1942.1 183.5 reduce-scatter.33
  2128.6 181.6 reduce-scatter.27
  2313.1 177.9 reduce-scatter.31
  2494.0 178.6 reduce-scatter.29
  2675.7 179.2 reduce-scatter.43
  2857.3 199.2 reduce-scatter.39
  3059.2 198.6 reduce-scatter.37
  3260.4 195.7 reduce-scatter.35
where the time goes:
time: 3500 us; the launch traced here: 3470 us
  waiting for transfers between devices  2870 us (82%)
  matrix products  216 us (6%)
  other arithmetic  122 us (3%)
  blocking collectives  107 us (3%)
  local copies, waits for them, and re-layouts  106 us (3%)
    unnamed x26, waiting for transfers between devices  672 us
    reduce_scatter x1, waiting for transfers between devices, local(): lax.psum_scatter(grad_w_down.astype(jnp.bfloat16), 'ctx', scatter_dimensi...  200 us
    reduce_scatter x1, waiting for transfers between devices, local(): lax.psum_scatter(grad_w_up.astype(jnp.bfloat16), 'ctx', scatter_dimension...  199 us
    reduce_scatter x1, waiting for transfers between devices, local(): lax.psum_scatter(grad_w_gate.astype(jnp.bfloat16), 'ctx', scatter_dimensi...  197 us
    reduce_scatter x1, waiting for transfers between devices, local(): lax.psum_scatter(grad_keys_all.astype(jnp.bfloat16), 'ctx', scatter_dimen...  188 us
    reduce_scatter x1, waiting for transfers between devices, local(): lax.psum_scatter(grad_w_attn_out.astype(jnp.bfloat16), 'ctx', scatter_dim...  184 us
    reduce_scatter x1, waiting for transfers between devices, local(): lax.psum_scatter(grad_w_query.astype(jnp.bfloat16), 'ctx', scatter_dimens...  183 us
    reduce_scatter x1, waiting for transfers between devices, local(): lax.psum_scatter(grad_w_key.astype(jnp.bfloat16), 'ctx', scatter_dimensio...  180 us
  transfers between devices with their start and end apart: 26, of which 24 were waited for; matrix products, arithmetic and copies ran while one was open for 4% of the time, Pallas kernels for 0%

commit v1 on v0

v1 whole, which is shorter than its diff:
```python
import jax
import jax.numpy as jnp
from jax import lax
from jax.experimental import pallas as pl
from jax.experimental.pallas import tpu as pltpu
from jax.sharding import PartitionSpec as P

EPS = 1e-06
ROPE_BASE = 1000000.0
ROOT_HALF = 0.7071067811865476
GELU_A = 0.7978845608028654
GELU_B = 0.044715
STRETCH = 128
HEAD = 256
SLOTS = 64
PAD_SLOTS = 72
CHUNK = 4
BF = jnp.bfloat16
F32 = jnp.float32


def hop(value, axis, mask):
    return lax.ppermute(value, axis, [(i, i ^ mask) for i in range(lax.axis_size(axis))])


def pick(value, index, axis):
    return lax.dynamic_index_in_dim(value, index, axis, keepdims=False)


def gather_wt(own):
    near = hop(own, "wt", 2)
    core = hop(own, "wt", 1)
    far = hop(near, "wt", 1)
    return own, near, core, far


def scatter_wt(part):
    half = part.shape[0] // 2
    quarter = half // 2
    kept = part[:half] + hop(part[half:].astype(BF), "wt", 1).astype(F32)
    return kept[:quarter] + hop(kept[quarter:].astype(BF), "wt", 2).astype(F32)


def scatter_axis(value, me, axis, unit, size):
    total = pick(value, me, axis).astype(F32)
    for k in range(1, size):
        total = total + hop(pick(value, me ^ k, axis).astype(BF), "ctx", k * unit).astype(F32)
    return total


def swap_halves(value):
    half = value.shape[0] // 2
    return jnp.concatenate([value[half:], value[:half]], axis=0)


def dot(left, right):
    return jnp.dot(left, right, preferred_element_type=F32)


def dot_rows(left, right):
    return lax.dot_general(left, right, (((0,), (0,)), ((), ())), preferred_element_type=F32)


def dot_cols(left, right):
    return lax.dot_general(left, right, (((1,), (1,)), ((), ())), preferred_element_type=F32)


def fine(left, right):
    return jnp.dot(
        left.astype(F32), right.astype(F32), precision=lax.Precision.HIGH, preferred_element_type=F32
    )


def fine_cols(left, right):
    return lax.dot_general(
        left.astype(F32),
        right.astype(F32),
        (((1,), (1,)), ((), ())),
        precision=lax.Precision.HIGH,
        preferred_element_type=F32,
    )


def rms(values):
    return lax.rsqrt(jnp.mean(values * values, axis=-1, keepdims=True) + EPS)


def norm_back(grad, normal, scale, gain):
    inner = grad * gain
    back = scale * (inner - normal * jnp.mean(inner * normal, axis=-1, keepdims=True))
    return back, jnp.sum(grad * normal, axis=0)


def rotate(values, cosine, sine):
    half = values.shape[-1] // 2
    front, rear = values[..., :half], values[..., half:]
    return jnp.concatenate([front * cosine - rear * sine, rear * cosine + front * sine], axis=-1)


def gelu_parts(value):
    square = value * value
    bend = jnp.tanh(GELU_A * value * (1.0 + GELU_B * square))
    half = 0.5 * (1.0 + bend)
    slope = half + 0.5 * value * (1.0 - bend * bend) * GELU_A * (1.0 + 3.0 * GELU_B * square)
    return value * half, slope


AT_V = PAD_SLOTS
AT_HI = 2 * PAD_SLOTS
AT_LO = AT_HI + 2
AT_Z = AT_LO + 2
AT_ENDS = AT_Z + 1


def load_pieces(pieces, held, sem):
    copies = [
        pltpu.make_async_copy(piece, held.at[pl.ds(8 * i, 8)], sem.at[i])
        for i, piece in enumerate(pieces)
    ]
    for copy in copies:
        copy.start()
    for copy in copies:
        copy.wait()


def query_places(meta, tile, shape, along):
    row = lax.broadcasted_iota(jnp.int32, shape, along) & (STRETCH - 1)
    row = (row + 64 * meta[AT_Z]) & (STRETCH - 1)
    place = meta[AT_HI + tile] * STRETCH + row
    start = jnp.zeros(shape, jnp.int32)
    for j in range(8):
        end = meta[AT_ENDS + j]
        start = jnp.maximum(start, jnp.where(place >= end, end, 0))
    return place, start


def key_places(meta, first, shape, along):
    at = lax.broadcasted_iota(jnp.int32, shape, along)
    row = ((at & (STRETCH - 1)) + 64 * meta[AT_Z]) & (STRETCH - 1)
    return first * STRETCH + (at - (at & (STRETCH - 1))) + row


def tile_of(ref, tile):
    rows = pl.ds(tile * STRETCH, STRETCH)
    return jnp.concatenate([ref[rows, :HEAD], ref[rows, HEAD:]], axis=0)


def stretches(meta, held, at, first):
    return jnp.concatenate([held[meta[at + first + u]] for u in range(CHUNK)], axis=0)


def turns_of(meta, tile):
    return (meta[AT_HI + tile] - meta[AT_LO + tile] + CHUNK) // CHUNK


def forward_kernel(meta, q_ref, *refs):
    pieces, (low_ref, full_ref, lse_ref), (held, acc, total, sem) = refs[:16], refs[16:19], refs[19:]
    load_pieces(pieces, held, sem)
    for tile in range(2):
        query = tile_of(q_ref, tile)
        place, start = query_places(meta, tile, (2 * STRETCH, 1), 0)
        acc[...] = jnp.zeros_like(acc)
        total[...] = jnp.zeros_like(total)

        def turn(i, carry):
            first = meta[AT_LO + tile] + CHUNK * i
            keys = stretches(meta, held, 0, first)
            values = stretches(meta, held, AT_V, first)
            scores = dot_cols(query, keys)
            key_at = key_places(meta, first, (1, CHUNK * STRETCH), 1)
            allowed = (key_at <= place) & (key_at >= start)
            weights = jnp.where(allowed, jnp.exp(scores), 0.0)
            part = weights[:, :STRETCH]
            for u in range(1, CHUNK):
                part = part + weights[:, u * STRETCH : (u + 1) * STRETCH]
            total[...] += part
            acc[...] += dot(weights.astype(BF), values)
            return carry

        lax.fori_loop(0, turns_of(meta, tile), turn, 0)
        row_total = jnp.sum(total[...], axis=1, keepdims=True)
        result = acc[...] / row_total
        rows = pl.ds(tile * STRETCH, STRETCH)
        for head in range(2):
            block = result[head * STRETCH : (head + 1) * STRETCH]
            low_ref[rows, head * HEAD : (head + 1) * HEAD] = block.astype(BF)
            full_ref[rows, head * HEAD : (head + 1) * HEAD] = block
        logs = jnp.broadcast_to(jnp.log(row_total), (2 * STRETCH, STRETCH))
        lse_ref[tile] = jnp.transpose(logs)[:8]


def backward_kernel(meta, q_ref, g_ref, full_ref, lse_ref, *refs):
    pieces, dq_ref, outs = refs[:16], refs[16], refs[17:33]
    held, grads, acc, sem = refs[33:]
    grads[...] = jnp.zeros_like(grads)
    load_pieces(pieces, held, sem)
    for tile in range(2):
        query = tile_of(q_ref, tile)
        grad = tile_of(g_ref, tile)
        full = tile_of(full_ref, tile)
        place, start = query_places(meta, tile, (1, 2 * STRETCH), 1)
        lse = lse_ref[tile][:1]
        delta = jnp.sum(grad.astype(F32) * full, axis=1, keepdims=True)
        delta = jnp.transpose(jnp.broadcast_to(delta, (2 * STRETCH, STRETCH)))[:1]
        acc[...] = jnp.zeros_like(acc)

        def turn(i, carry):
            first = meta[AT_LO + tile] + CHUNK * i
            keys = stretches(meta, held, 0, first)
            values = stretches(meta, held, AT_V, first)
            key_at = key_places(meta, first, (CHUNK * STRETCH, 1), 0)
            allowed = (key_at <= place) & (key_at >= start)
            weights = jnp.where(allowed, jnp.exp(dot_cols(keys, query) - lse), 0.0)
            slopes = (weights * (dot_cols(values, grad) - delta)).astype(BF)
            key_term = dot(slopes, query)
            value_term = dot(weights.astype(BF), grad)
            acc[...] += dot_rows(slopes, keys)
            for u in range(CHUNK):
                part = slice(u * STRETCH, (u + 1) * STRETCH)
                for at, term in ((meta[first + u], key_term), (meta[AT_V + first + u], value_term)):
                    grads[at] = (grads[at].astype(F32) + term[part]).astype(BF)
            return carry

        lax.fori_loop(0, turns_of(meta, tile), turn, 0)
        rows = pl.ds(tile * STRETCH, STRETCH)
        for head in range(2):
            block = acc[head * STRETCH : (head + 1) * STRETCH]
            dq_ref[rows, head * HEAD : (head + 1) * HEAD] = block * (HEAD**-0.5)
    copies = [
        pltpu.make_async_copy(grads.at[pl.ds(8 * i, 8)], out, sem.at[i])
        for i, out in enumerate(outs)
    ]
    for copy in copies:
        copy.start()
    for copy in copies:
        copy.wait()


def in_vmem():
    return pl.BlockSpec(memory_space=pltpu.VMEM)


def anywhere():
    return pl.BlockSpec(memory_space=pl.ANY)


def attend_forward(meta, query, pieces):
    rows = query.shape[0]
    return pl.pallas_call(
        forward_kernel,
        out_shape=(
            jax.ShapeDtypeStruct((rows, 2 * HEAD), BF),
            jax.ShapeDtypeStruct((rows, 2 * HEAD), F32),
            jax.ShapeDtypeStruct((2, 8, 2 * STRETCH), F32),
        ),
        in_specs=[pl.BlockSpec(memory_space=pltpu.SMEM), in_vmem()] + [anywhere()] * 16,
        out_specs=(in_vmem(), in_vmem(), in_vmem()),
        scratch_shapes=[
            pltpu.VMEM((2 * SLOTS, STRETCH, HEAD), BF),
            pltpu.VMEM((2 * STRETCH, HEAD), F32),
            pltpu.VMEM((2 * STRETCH, STRETCH), F32),
            pltpu.SemaphoreType.DMA((16,)),
        ],
        compiler_params=pltpu.CompilerParams(vmem_limit_bytes=24 * 1024 * 1024),
        cost_estimate=pl.CostEstimate(
            flops=3 * 10**9, bytes_accessed=10**7, transcendentals=2 * 10**6
        ),
        name="attend_forward",
    )(meta, query, *pieces)


def attend_backward(meta, query, grad, full, lse, pieces):
    rows = query.shape[0]
    piece = jax.ShapeDtypeStruct((8, STRETCH, HEAD), BF)
    outs = pl.pallas_call(
        backward_kernel,
        out_shape=(jax.ShapeDtypeStruct((rows, 2 * HEAD), F32),) + (piece,) * 16,
        in_specs=[pl.BlockSpec(memory_space=pltpu.SMEM)] + [in_vmem()] * 4 + [anywhere()] * 16,
        out_specs=(in_vmem(),) + (anywhere(),) * 16,
        scratch_shapes=[
            pltpu.VMEM((2 * SLOTS, STRETCH, HEAD), BF),
            pltpu.VMEM((2 * SLOTS, STRETCH, HEAD), BF),
            pltpu.VMEM((2 * STRETCH, HEAD), F32),
            pltpu.SemaphoreType.DMA((16,)),
        ],
        compiler_params=pltpu.CompilerParams(vmem_limit_bytes=36 * 1024 * 1024),
        cost_estimate=pl.CostEstimate(
            flops=10**10, bytes_accessed=2 * 10**7, transcendentals=2 * 10**6
        ),
        name="attend_backward",
    )(meta, query, grad, full, lse, *pieces)
    return outs[0], outs[1:]


def local(
    stream,
    layer_input,
    out_grad,
    doc_lengths,
    stretch_slots,
    gain_input,
    gain_query,
    gain_key,
    w_query,
    w_key,
    w_value,
    w_attn_out,
    gain_attn,
    laurel_left,
    laurel_right,
    gain_laurel,
    gain_pre_ff,
    w_gate,
    w_up,
    w_down,
    gain_post_ff,
    join_gate,
    join_proj,
    gain_join,
):
    wt = lax.axis_index("wt")
    core, zlo = wt & 1, wt >> 1
    ctx = lax.axis_index("ctx")
    at_x, at_z, at_y = ctx & 3, (ctx >> 2) & 1, ctx >> 3
    first_core = core == 0
    half = HEAD // 2

    def starts(k):
        return ((core ^ (k & 1)) * 2 + (zlo ^ (k >> 1))) * 64

    def natural(blocks):
        stacked = jnp.stack(blocks)
        return jnp.concatenate(
            [pick(stacked, wt ^ ((b & 1) * 2 + (b >> 1)), 0) for b in range(4)], axis=0
        )

    stream_f = jnp.concatenate(
        [lax.dynamic_slice_in_dim(stream, starts(k), 64, 0) for k in (0, 2, 1, 3)], axis=0
    ).astype(F32)
    grad_top = lax.dynamic_slice_in_dim(out_grad, starts(0), 64, 0).astype(F32)

    pack = jnp.concatenate([laurel_left.T, laurel_right, join_gate.T, join_proj], axis=0)
    packs = [pack] + [hop(pack, "wt", k) for k in (1, 2, 3)]
    left_t = jnp.concatenate([p[:16] for p in packs], axis=0)
    right_w = jnp.concatenate([p[16:32] for p in packs], axis=0)
    gate_t = jnp.concatenate([p[32:96] for p in packs], axis=0)
    proj_w = jnp.concatenate([p[96:160] for p in packs], axis=0)
    inputs = [lax.dynamic_slice_in_dim(layer_input, starts(k), 64, 0) for k in range(4)]
    input_f = jnp.concatenate(
        [inputs[0]] + [hop(inputs[k], "wt", k) for k in (1, 2, 3)], axis=1
    ).astype(F32)

    doc_ends = jnp.cumsum(doc_lengths)
    tiles = [lax.dynamic_index_in_dim(stretch_slots, 2 * ctx + (core ^ t), 0) for t in range(2)]
    hi = jnp.concatenate(tiles)
    lo = jnp.max(
        jnp.where(doc_ends[None, :] <= hi[:, None] * STRETCH, doc_ends[None, :], 0), axis=1
    )
    lo = lo // STRETCH
    row = (jnp.arange(STRETCH, dtype=jnp.int32) + 64 * zlo) & (STRETCH - 1)
    positions = (hi[:, None] * STRETCH + row[None, :]).reshape(-1)
    names = jnp.arange(SLOTS, dtype=jnp.int32)
    slot_of = jnp.sum(jnp.where(stretch_slots[None, :] == names[:, None], names[None, :], 0), axis=1)
    relative = (slot_of >> 1) ^ ctx
    rel_x, rel_z, rel_y = relative & 3, (relative >> 2) & 1, relative >> 3
    places = (
        rel_y * 8 + rel_x * 2 + rel_z,
        SLOTS // 2 + rel_x * 8 + rel_y * 2 + rel_z,
    )
    second = (slot_of & 1) == 1
    key_at = core * SLOTS + jnp.where(second, places[1], places[0])
    value_at = (1 - core) * SLOTS + jnp.where(second, places[0], places[1])
    blank = jnp.zeros((PAD_SLOTS - SLOTS,), jnp.int32)
    meta = jnp.concatenate([key_at, blank, value_at, blank, hi, lo, zlo[None], doc_ends]).astype(
        jnp.int32
    )
    exponents = jnp.arange(half, dtype=F32) * (2.0 / HEAD)
    angles = positions.astype(F32)[:, None] * (1.0 / ROPE_BASE**exponents)[None, :]
    cosine, sine = jnp.cos(angles), jnp.sin(angles)

    scale_in = rms(stream_f)
    normal_in = stream_f * scale_in
    normed = normal_in * gain_input
    normed_b = normed.astype(BF)
    key_half = dot(normed_b, w_key)
    value_half = dot(normed_b, w_value)
    arrived = swap_halves(hop(jnp.where(first_core, value_half, key_half), "wt", 1))
    kind = jnp.concatenate(
        [jnp.where(first_core, key_half, arrived), jnp.where(first_core, arrived, value_half)],
        axis=1,
    )
    kind_gain = jnp.where(first_core, gain_key, 1.0)
    kind_cos = jnp.where(first_core, cosine, 1.0)
    kind_sin = jnp.where(first_core, sine, 0.0)
    kind_scale = rms(kind)
    kind_normal = kind * kind_scale
    kind_b = rotate(kind_normal * kind_gain, kind_cos, kind_sin).astype(BF)

    across = hop(kind_b, "ctx", 4)
    pieces = []
    for h, (one, two) in enumerate(((1, 8), (8, 1))):
        rows = slice(h * STRETCH, (h + 1) * STRETCH)
        block = jnp.concatenate([kind_b[rows], across[rows]], axis=0)
        block = jnp.concatenate([block] + [hop(block, "ctx", k * one) for k in (1, 2, 3)], axis=0)
        pieces += [block] + [hop(block, "ctx", k * two) for k in (1, 2, 3)]
    pieces += [hop(piece, "wt", 1) for piece in pieces]
    pieces = [piece.reshape(8, STRETCH, HEAD) for piece in pieces]

    query_raw = dot(normed_b, w_query).reshape(2 * STRETCH, 2, HEAD)
    query_scale = rms(query_raw)
    query_normal = query_raw * query_scale
    query_rot = rotate(query_normal * gain_query, cosine[:, None, :], sine[:, None, :])
    query_b = (query_rot.astype(BF) * (HEAD**-0.5)).astype(BF).reshape(2 * STRETCH, 2 * HEAD)

    attn_b, attn_full, lse = attend_forward(meta, query_b, pieces)

    attn_sum = scatter_wt(dot(attn_b, w_attn_out))
    stream_own, normed_own, normed_own_b = stream_f[:64], normed[:64], normed_b[:64]
    normal_own = normal_in[:64]
    laurel_mid = fine_cols(normed_own_b, left_t)
    laurel_sum = fine(laurel_mid, right_w)
    attn_scale, laurel_scale = rms(attn_sum), rms(laurel_sum)
    attn_normal, laurel_normal = attn_sum * attn_scale, laurel_sum * laurel_scale
    residual = (
        stream_own + attn_normal * gain_attn + normed_own + laurel_normal * gain_laurel
    ) * ROOT_HALF
    pre_scale = rms(residual)
    pre_normal = residual * pre_scale
    pre_all = jnp.concatenate(gather_wt((pre_normal * gain_pre_ff).astype(BF)), axis=0)

    gate_pre = dot(pre_all, w_gate)
    up_pre = dot(pre_all, w_up)
    act_b = (gelu_parts(gate_pre)[0] * up_pre).astype(BF)
    ff_sum = scatter_wt(dot(act_b, w_down))
    pre_group = jnp.concatenate([pre_all] + [hop(pre_all, "ctx", k) for k in (1, 2, 3)], axis=0)
    act_group = jnp.concatenate([act_b] + [hop(act_b, "ctx", 8 * k) for k in (1, 2, 3)], axis=0)
    ff_scale = rms(ff_sum)
    ff_normal = ff_sum * ff_scale
    after_ff = residual + ff_normal * gain_post_ff

    join_pre = fine_cols(after_ff, gate_t)
    join_gelu, join_slope = gelu_parts(join_pre)
    joined = join_gelu * input_f
    join_sum = fine(joined, proj_w)
    join_scale = rms(join_sum)
    join_normal = join_sum * join_scale
    layer_out = after_ff + join_normal * gain_join

    grad_join_sum, gain_join_part = norm_back(grad_top, join_normal, join_scale, gain_join)
    grad_joined = fine_cols(grad_join_sum, proj_w)
    grad_join_pre = grad_joined * input_f * join_slope
    grad_input = grad_joined * join_gelu
    grad_after = grad_top + fine(grad_join_pre, gate_t)

    grad_ff, gain_post_part = norm_back(grad_after, ff_normal, ff_scale, gain_post_ff)
    grad_ff_all = jnp.concatenate(gather_wt(grad_ff.astype(BF)), axis=0)
    grad_act = dot_cols(grad_ff_all, w_down)
    gate_gelu, gate_slope = gelu_parts(gate_pre)
    grad_gate_b = (grad_act * up_pre * gate_slope).astype(BF)
    grad_up_b = (grad_act * gate_gelu).astype(BF)
    grad_pre = scatter_wt(dot_cols(grad_gate_b, w_gate) + dot_cols(grad_up_b, w_up))

    grad_resid, gain_pre_part = norm_back(grad_pre, pre_normal, pre_scale, gain_pre_ff)
    branch = (grad_after + grad_resid) * ROOT_HALF
    grad_attn, gain_attn_part = norm_back(branch, attn_normal, attn_scale, gain_attn)
    grad_attn_all = jnp.concatenate(gather_wt(grad_attn.astype(BF)), axis=0)
    grad_heads = dot_cols(grad_attn_all, w_attn_out).astype(BF)
    grad_laurel, gain_laurel_part = norm_back(branch, laurel_normal, laurel_scale, gain_laurel)
    grad_mid = fine_cols(grad_laurel, right_w)

    grad_query_rot, grad_pieces = attend_backward(
        meta, query_b, grad_heads, attn_full, lse, pieces
    )
    kind_rows = []
    for h, (one, two) in enumerate(((1, 8), (8, 1))):
        own = [
            grad_pieces[4 * h + j].astype(F32)
            + hop(grad_pieces[8 + 4 * h + j], "wt", 1).astype(F32)
            for j in range(4)
        ]
        total = own[0]
        for k in (1, 2, 3):
            total = total + hop(own[k].astype(BF), "ctx", k * two).astype(F32)
        total = total.reshape(4, 2, STRETCH, HEAD)
        sums = total[0]
        for k in (1, 2, 3):
            sums = sums + hop(total[k].astype(BF), "ctx", k * one).astype(F32)
        kind_rows.append(sums[0] + hop(sums[1].astype(BF), "ctx", 4).astype(F32))
    grad_kind_rot = jnp.concatenate(kind_rows, axis=0)
    grad_kind_normed = rotate(grad_kind_rot, kind_cos, -kind_sin)
    grad_kind, gain_kind_part = norm_back(grad_kind_normed, kind_normal, kind_scale, kind_gain)
    gain_key_part = jnp.where(first_core, gain_kind_part, 0.0)
    away = jnp.where(first_core, grad_kind[:, half:], grad_kind[:, :half]).astype(BF)
    home = jnp.where(first_core, grad_kind[:, :half], grad_kind[:, half:]).astype(BF)
    away = swap_halves(hop(away, "wt", 1))
    grad_key_b = jnp.where(first_core, home, away)
    grad_value_b = jnp.where(first_core, away, home)

    grad_query_normed = rotate(
        grad_query_rot.reshape(2 * STRETCH, 2, HEAD), cosine[:, None, :], -sine[:, None, :]
    )
    grad_query, gain_query_part = norm_back(
        grad_query_normed, query_normal, query_scale, gain_query
    )
    gain_query_part = jnp.sum(gain_query_part, axis=0)
    grad_query_b = grad_query.astype(BF).reshape(2 * STRETCH, 2 * HEAD)

    normed_part = (
        dot_cols(grad_query_b, w_query)
        + dot_cols(grad_key_b, w_key)
        + dot_cols(grad_value_b, w_value)
    )
    own_part = branch + fine(grad_mid, left_t)
    gain_input_part = jnp.sum(own_part * normal_own, axis=0) + jnp.sum(
        normed_part * normal_in, axis=0
    )
    grad_normed = own_part + scatter_wt(normed_part)
    grad_stream_extra, _ = norm_back(grad_normed, normal_own, scale_in[:64], gain_input)
    stream_grad = branch + grad_stream_extra

    def spread(own):
        first, near, core_rows, far = gather_wt(own.astype(BF))
        return natural([first, core_rows, near, far]).astype(F32)

    layer_out_all = spread(layer_out)
    stream_grad_all = spread(stream_grad)
    parts = [grad_input[:, 64 * k : 64 * (k + 1)] for k in range(4)]
    grad_input_all = natural([parts[0]] + [hop(parts[k], "wt", k) for k in (1, 2, 3)])

    def scatter_ctx(grad, order):
        value = grad.astype(BF).reshape(4, 2, 4, 64, -1)
        if order == "x":
            value = scatter_axis(value, at_x, 2, 1, 4).astype(BF)
            value = scatter_axis(value, at_y, 0, 8, 4).astype(BF)
        else:
            value = scatter_axis(value, at_y, 0, 8, 4).astype(BF)
            value = scatter_axis(value, at_x, 1, 1, 4).astype(BF)
        return scatter_axis(value, at_z, 0, 4, 2)

    quarter = 512
    ff_group = [
        lax.dynamic_slice_in_dim(grad_ff_all, (at_y ^ k) * quarter, quarter, 1) for k in range(4)
    ]
    ff_group = jnp.concatenate(
        [ff_group[0]] + [hop(ff_group[k], "ctx", 8 * k) for k in (1, 2, 3)], axis=0
    )
    down = dot_rows(ff_group, act_group).astype(BF).reshape(2, 4, 64, -1)
    down = scatter_axis(down, at_x, 1, 1, 4).astype(BF)
    grad_w_down = scatter_axis(down, at_z, 0, 4, 2).T

    wide = []
    for grad in (grad_gate_b, grad_up_b):
        cuts = [
            lax.dynamic_slice_in_dim(grad, (at_x ^ k) * quarter, quarter, 1) for k in range(4)
        ]
        cuts = jnp.concatenate([cuts[0]] + [hop(cuts[k], "ctx", k) for k in (1, 2, 3)], axis=0)
        value = dot_rows(pre_group, cuts).astype(BF).reshape(4, 2, 4, 64, quarter)
        value = scatter_axis(value, at_y, 0, 8, 4).astype(BF)
        value = scatter_axis(value, at_z, 0, 4, 2).astype(BF)
        got = [pick(value, at_x, 0)]
        got += [hop(pick(value, at_x ^ k, 0), "ctx", k) for k in (1, 2, 3)]
        stacked = jnp.stack(got)
        wide.append(
            jnp.concatenate([pick(stacked, at_x ^ q, 0) for q in range(4)], axis=1).astype(F32)
        )
    grad_w_gate, grad_w_up = wide

    grad_w_attn_out = scatter_ctx(dot_rows(grad_attn_all, attn_b), "y").T
    grad_w_query = scatter_ctx(dot_rows(normed_b, grad_query_b), "x")
    pair = jnp.concatenate([grad_key_b, grad_value_b], axis=1)
    grad_pair = scatter_ctx(dot_rows(normed_b, pair), "y")
    grad_w_key, grad_w_value = grad_pair[:, :half], grad_pair[:, half:]

    low = [
        dot_rows(grad_mid.astype(BF), normed_own_b),
        dot_rows(laurel_mid.astype(BF), grad_laurel.astype(BF)),
        dot_rows(grad_join_pre.astype(BF), after_ff.astype(BF)),
        dot_rows(joined.astype(BF), grad_join_sum.astype(BF)),
    ]
    gains = jnp.stack(
        [gain_attn_part, gain_laurel_part, gain_pre_part, gain_post_part, gain_join_part]
        + [jnp.zeros_like(gain_attn_part)] * 3
    )

    def small_block(k):
        return [value[value.shape[0] // 4 * k :][: value.shape[0] // 4] for value in low] + [gains]

    small = jnp.concatenate(
        small_block(0) + small_block(2) + small_block(1) + small_block(3), axis=0
    )
    small = scatter_ctx(scatter_wt(small).T, "x")
    grad_left, grad_right = small[:, :16], small[:, 16:32].T
    grad_gate, grad_proj = small[:, 32:96], small[:, 96:160].T

    late = jnp.concatenate(
        [
            gain_input_part.reshape(32, 64),
            gain_query_part.reshape(32, 8),
            gain_key_part.reshape(32, 8),
            jnp.zeros((32, 48), F32),
        ],
        axis=1,
    ).reshape(4, 2, 4, 128)
    for axis, me, unit, size in ((2, at_x, 1, 4), (0, at_y, 8, 4), (0, at_z, 4, 2)):
        total = pick(late, me, axis)
        for k in range(1, size):
            total = total + hop(pick(late, me ^ k, axis), "ctx", k * unit)
        late = total
    late = late + hop(late, "wt", 1)
    late = late + hop(late, "wt", 2)

    return (
        layer_out_all,
        stream_grad_all,
        grad_input_all,
        late[:64],
        late[64:72],
        late[72:80],
        grad_w_query,
        grad_w_key,
        grad_w_value,
        grad_w_attn_out,
        small[:, 160],
        grad_left,
        grad_right,
        small[:, 161],
        small[:, 162],
        grad_w_gate,
        grad_w_up,
        grad_w_down,
        small[:, 163],
        grad_gate,
        grad_proj,
        small[:, 164],
    )


def solution(mesh):
    rows, cols, tops = P("ctx", "wt"), P("wt", "ctx"), P("ctx")
    down, across = P(None, "wt"), P("wt", None)
    return jax.shard_map(
        local,
        mesh=mesh,
        in_specs=(
            P("ctx", None),
            P("ctx", "wt"),
            P("ctx", None),
            P(),
            P(),
            P(),
            P(),
            P(),
            down,
            down,
            down,
            across,
            P(),
            down,
            across,
            P(),
            P(),
            down,
            down,
            across,
            P(),
            down,
            across,
            P(),
        ),
        out_specs=(
            P("ctx", None),
            P("ctx", None),
            rows,
            tops,
            tops,
            tops,
            rows,
            rows,
            rows,
            cols,
            tops,
            rows,
            cols,
            tops,
            tops,
            rows,
            rows,
            cols,
            tops,
            rows,
            cols,
            tops,
        ),
        check_vma=False,
    )
```

time: 3500 us -> 675 us (0.19)
  waiting for transfers between devices: 2870 us -> 174 us
  starting transfers between devices: 28.1 us -> 233 us
  matrix products: 216 us -> 59.1 us
  blocking collectives: 107 us -> 0 us
  other arithmetic: 122 us -> 63.3 us
    reduce_scatter x10 -> x0, waiting for transfers between devices: 1740 us -> none  [the longest x1 200 us: local(): lax.psum_scatter(grad_w_down.astype(jnp.bfloat16), 'ctx', scatter_dimensi...]
    unnamed x26 -> x0, waiting for transfers between devices: 672 us -> none
    psum x6 -> x0, waiting for transfers between devices: 320 us -> none  [the longest x1 89.8 us: local(): attn_sum, laurel_sum = lax.psum((attn_part, laurel_part), 'wt')]
    ppermute x4 -> x149, starting transfers between devices: 25.7 us -> 233 us  [hop(): lax.ppermute(value, axis, [(i, i ^ mask) for i in range(lax.axis_size(axi...]
    ppermute x4 -> x149, waiting for transfers between devices: 1.37 us -> 174 us  [hop(): lax.ppermute(value, axis, [(i, i ^ mask) for i in range(lax.axis_size(axi...]
    dot_general x105 -> x32, matrix products: 216 us -> 59.1 us  [the longest x7 22.2 us: dot_cols(): lax.dot_general(left, right, (((1,), (1,)), ((), ())), preferred_element_...]
    all_gather x2 -> x0, waiting for transfers between devices: 135 us -> none  [the longest x1 75.9 us: local(): lax.all_gather(key_b, 'ctx', axis=0, tiled=True)]
    unnamed x1 -> x0, blocking collectives: 77.1 us -> none
  transfers between devices with their start and end apart: 26 -> 149, of which waited for: 24 -> 43; matrix products, arithmetic and copies ran while one was open for 4% -> 32% of each run, Pallas kernels for 0% -> 2%
where the time goes in v1:
time: 675 us; the launch traced here: 664 us
  starting transfers between devices  233 us (35%)
  waiting for transfers between devices  174 us (26%)
  local copies, waits for them, and re-layouts  116 us (17%)
  other arithmetic  63.3 us (9%)
  matrix products  59.1 us (9%)
  Pallas kernels  13.7 us (2%)
    ppermute x149, starting transfers between devices, hop(): lax.ppermute(value, axis, [(i, i ^ mask) for i in range(lax.axis_size(axi...  233 us
    ppermute x149, waiting for transfers between devices, hop(): lax.ppermute(value, axis, [(i, i ^ mask) for i in range(lax.axis_size(axi...  174 us
    unnamed x395, local copies, waits for them, and re-layouts  37.4 us
    concatenate x2, local copies, waits for them, and re-layouts, local(): jnp.concatenate(small_block(0) + small_block(2) + small_block(1) + small_...  30.6 us
    dot_general x7, matrix products, dot_cols(): lax.dot_general(left, right, (((1,), (1,)), ((), ())), preferred_element_...  22.2 us
    dot_general x10, matrix products, dot_rows(): lax.dot_general(left, right, (((0,), (0,)), ((), ())), preferred_element_...  15.9 us
    dot_general x7, matrix products, dot(): return jnp.dot(left, right, preferred_element_type=F32)  14 us
  transfers between devices with their start and end apart: 149, of which 43 were waited for; matrix products, arithmetic and copies ran while one was open for 32% of the time, Pallas kernels for 2%

profile of v1, /device:TPU:1, one launch (start us, length us, event | category | flops | bytes accessed | tf_op | source)
XLA Modules:
  0.0 664.1 jit_solution(12772921665998506928)
XLA Ops:
  2.8 3.0 collective-permute-start.26
  10.8 2.8 maximum_convert_fusion
  24.0 3.4 collective-permute-start.1
  32.9 2.7 collective-permute-start.9
  35.6 2.6 collective-permute-start.4
  40.2 3.9 collective-permute-done.10
  44.1 3.9 collective-permute-start.18
  53.8 3.1 collective-permute-done.25
  56.8 4.7 collective-permute-start.14
  75.2 2.5 collective-permute-start.5
  81.0 19.7 %collective-permute-done.7 = bf16[1024,256]{1,0:T(8,128)(2,1)S(1)} collective-permute-done((bf16[1024,256]{1,0:T(8,128)(2,1)}, bf16[1024,256]{1,0:T(8,128)(2,1)S(1)}, u32[]{:S(2)}, u32[]{:S(2)}) %collective-permute-start.7) | collective-permute-done | bytes 524320 | tf_op jit(solution)/shard_map/ppermute | solution.py:23
  108.1 5.5 attend_forward.1
  117.4 7.0 %collective-permute-done.23 = bf16[64,2048]{1,0:T(8,128)(2,1)S(1)} collective-permute-done((bf16[64,2048]{1,0:T(8,128)(2,1)S(1)}, bf16[64,2048]{1,0:T(8,128)(2,1)S(1)}, u32[]{:S(2)}, u32[]{:S(2)}) %collective-permute-start.23) | collective-permute-done | bytes 262176 | tf_op jit(solution)/shard_map/ppermute | solution.py:23
  130.5 3.8 collective-permute-done.27
  140.3 4.3 multiply_convert_fusion.2
  144.6 3.5 fusion.192
  153.6 4.8 collective-permute-done.31
  160.0 2.7 collective-permute-start.117
  172.3 8.6 %collective-permute-start.74 = (f32[64,64]{1,0:T(8,128)S(1)}, f32[64,64]{1,0:T(8,128)S(1)}, u32[]{:S(2)}, u32[]{:S(2)}) collective-permute-start(f32[64,64]{1,0:T(8,128)S(1)} %get-tuple-element.337), channel_id=1, source_target_pairs={{0,1},{1,0},{2,3},{3,2},{4,5},{5,4},{6,7},{7,6},{8,9},{9,8},{10,11... | collective-permute-start | bytes 49160 | tf_op jit(solution)/shard_map/ppermute | solution.py:23
  190.6 8.7 %collective-permute-done.117 = bf16[256,2048]{1,0:T(8,128)(2,1)} collective-permute-done((bf16[256,2048]{1,0:T(8,128)(2,1)}, bf16[256,2048]{1,0:T(8,128)(2,1)}, u32[]{:S(2)}, u32[]{:S(2)}) %collective-permute-start.117) | collective-permute-done | bytes 1048608 | tf_op jit(solution)/shard_map/ppermute | solution.py:23
  210.3 7.9 %multiply_convert_fusion = (bf16[256,2048]{1,0:T(8,128)(2,1)S(1)}, bf16[256,2048]{1,0:T(8,128)(2,1)S(1)}) fusion(f32[256,2048]{1,0:T(8,128)S(1)} %copy-done.177, f32[256,2048]{1,0:T(8,128)} %get-tuple-element.367, bf16[2048,2048]{1,0:T(8,128)(2,1)} %param.43, bf16[64,2048]{1,0:T(8,128)(2,1)S(1)} %collective-permute-done.40, ...), kind=kOutput, calls=%fused_computation.21 | convolution fusion | flops 2163212288 | bytes 15728640 | tf_op jit(solution)/shard_map/dot_general | solution.py:65
  223.5 5.7 convolution_add_fusion.2
  232.9 2.6 collective-permute-start.143
  235.5 5.1 collective-permute-done.121
  244.6 4.1 collective-permute-done.130
  248.8 2.9 collective-permute-start.140
  253.4 2.5 convolution_convert_fusion
  255.9 2.5 collective-permute-start.141
  258.7 3.8 collective-permute-start.41
  262.5 17.5 %collective-permute-done.142 = bf16[256,2048]{1,0:T(8,128)(2,1)S(1)} collective-permute-done((bf16[256,2048]{1,0:T(8,128)(2,1)}, bf16[256,2048]{1,0:T(8,128)(2,1)S(1)}, u32[]{:S(2)}, u32[]{:S(2)}) %collective-permute-start.142) | collective-permute-done | bytes 1048608 | tf_op jit(solution)/shard_map/ppermute | solution.py:23
  281.2 4.8 collective-permute-done.140
  288.1 3.2 collective-permute-done.139
  292.5 3.9 fusion.8
  298.1 4.0 collective-permute-done.42
  309.7 4.4 collective-permute-done.123
  318.3 6.7 %collective-permute-done.132 = bf16[2,4,64,512]{3,2,1,0:T(8,128)(2,1)S(1)} collective-permute-done((bf16[2,4,64,512]{3,2,1,0:T(8,128)(2,1)S(1)}, bf16[2,4,64,512]{3,2,1,0:T(8,128)(2,1)S(1)}, u32[]{:S(2)}, u32[]{:S(2)}) %collective-permute-start.132) | collective-permute-done | bytes 524320 | tf_op jit(solution)/shard_map/ppermute | solution.py:23
  327.4 4.4 collective-permute-start.44
  331.7 4.8 collective-permute-done.133
  343.4 6.8 %collective-permute-start.125 = (bf16[4,64,512]{2,1,0:T(8,128)(2,1)}, bf16[4,64,512]{2,1,0:T(8,128)(2,1)}, u32[]{:S(2)}, u32[]{:S(2)}) collective-permute-start(bf16[4,64,512]{2,1,0:T(8,128)(2,1)} %dynamic-slice_bitcast_fusion.14), channel_id=1, source_target_pairs={{0,16},{4,20},{8,24},{12,28},{16,0},{20,4},{24,8},{28,12},{32,48},... | collective-permute-start | bytes 786440 | tf_op jit(solution)/shard_map/ppermute | solution.py:23
  351.5 2.9 collective-permute-start.148
  355.8 16.2 %concatenate.165 = f32[336,2048]{1,0:T(8,128)} concatenate(f32[16,2048]{1,0:T(8,128)} %get-tuple-element.385, f32[16,2048]{1,0:T(8,128)} %get-tuple-element.267, f32[64,2048]{1,0:T(8,128)} %get-tuple-element.383, f32[64,2048]{1,0:T(8,128)} %get-tuple-element.198, f32[1,2048]{1,0:T(1,128)S(1)} %bitcast.416, f32[1,2048]{1,0:T(1,128)S(1)} %bitcast.413, f32[1,2048]{1,0:T(1,128)S(1)} %bitcast.410, ...), dimensions={0} | concatenate | bytes 5505024 | tf_op jit(solution)/shard_map/concatenate | solution.py:588
  373.7 14.5 %concatenate.166 = bf16[336,2048]{1,0:T(8,128)(2,1)} concatenate(bf16[16,2048]{1,0:T(8,128)(2,1)} %get-tuple-element.389, bf16[16,2048]{1,0:T(8,128)(2,1)} %get-tuple-element.308, bf16[64,2048]{1,0:T(8,128)(2,1)} %get-tuple-element.387, bf16[64,2048]{1,0:T(8,128)(2,1)} %get-tuple-element.230, bf16[1,2048]{1,0:T(2,128)(2,1)} %convert.145, bf16[1,2048]{1,0:T(2,128)(2,1)} %convert.146, ...), dimensions={0} | concatenate | bytes 2752512 | tf_op jit(solution)/shard_map/concatenate | solution.py:588
  398.9 4.8 collective-permute-start.45
  410.7 3.9 collective-permute-start.102
  416.6 8.2 %attend_backward.1 = (f32[256,512]{1,0:T(8,128)S(1)}, bf16[8,128,256]{2,1,0:T(8,128)(2,1)S(1)}, bf16[8,128,256]{2,1,0:T(8,128)(2,1)S(1)}, bf16[8,128,256]{2,1,0:...) custom-call(s32[157]{0:T(256)S(1)} %concatenate.136.meta, ...), custom_call_target="tpu_custom_call" | custom-call | flops 10000000000 | bytes 20000000 | tf_op jit(solution)/shard_map/attend_backward/pallas_call | solution.py:275
  436.1 3.2 collective-permute-start.47
  454.2 4.6 collective-permute-done.105
  460.1 4.0 collective-permute-start.106
  467.1 3.7 collective-permute-start.52
  474.6 9.0 %collective-permute-done.50 = bf16[8,128,256]{2,1,0:T(8,128)(2,1)S(1)} collective-permute-done((bf16[8,128,256]{2,1,0:T(8,128)(2,1)S(1)}, bf16[8,128,256]{2,1,0:T(8,128)(2,1)S(1)}, u32[]{:S(2)}, u32[]{:S(2)}) %collective-permute-start.50) | collective-permute-done | bytes 524320 | tf_op jit(solution)/shard_map/ppermute | solution.py:23
  483.5 4.6 collective-permute-start.63
  488.2 5.0 collective-permute-done.52
  495.8 2.9 collective-permute-start.54
  498.7 13.1 %collective-permute-done.63 = bf16[8,128,256]{2,1,0:T(8,128)(2,1)S(1)} collective-permute-done((bf16[8,128,256]{2,1,0:T(8,128)(2,1)S(1)}, bf16[8,128,256]{2,1,0:T(8,128)(2,1)S(1)}, u32[]{:S(2)}, u32[]{:S(2)}) %collective-permute-start.63) | collective-permute-done | bytes 524320 | tf_op jit(solution)/shard_map/ppermute | solution.py:23
  518.1 3.1 collective-permute-done.65
  523.4 2.8 collective-permute-done.67
  533.5 3.4 collective-permute-start.68
  559.2 6.2 collective-permute-done.95
  574.7 3.1 collective-permute-done.109
  581.2 2.9 collective-permute-done.110
  589.4 20.3 %collective-permute-start.69 = (bf16[128,2048]{1,0:T(8,128)(2,1)S(1)}, bf16[128,2048]{1,0:T(8,128)(2,1)S(1)}, u32[]{:S(2)}, u32[]{:S(2)}) collective-permute-start(bf16[128,2048]{1,0:T(8,128)(2,1)S(1)} %copy-done.108), channel_id=1, source_target_pairs={{0,1},{1,0},{2,3},{3,2},{4,5},{5,4},{6,7},{7,6},{8,9},{9,8},{10,11... | collective-permute-start | bytes 1572872 | tf_op jit(solution)/shard_map/ppermute | solution.py:23
  629.4 2.8 collective-permute-start.78
  645.0 7.3 %collective-permute-start.84 = (f32[128]{0:T(128)S(1)}, f32[128]{0:T(128)S(1)}, u32[]{:S(2)}, u32[]{:S(2)}) collective-permute-start(f32[128]{0:T(128)S(1)} %fusion.131), channel_id=1, source_target_pairs={{0,1},{1,0},{2,3},{3,2},{4,5},{5,4},{6,7},{7,6},{8,9},{9,8},{10,11... | collective-permute-start | bytes 1544 | tf_op jit(solution)/shard_map/ppermute | solution.py:23
  661.1 2.5 maximum_convert_fusion.1
  (886 shorter events, 306.3 us)
Async XLA Ops:
  2.8 47.7 %collective-permute-start.26 = (bf16[160,2048]{1,0:T(8,128)(2,1)}, bf16[160,2048]{1,0:T(8,128)(2,1)}, u32[]{:S(2)}, u32[]{:S(2)}) collective-permute-start(bf16[160,2048]{1,0:T(8,128)(2,1)} %pad_maximum_fusion.7), channel_id=1, source_target_pairs={{0,3},{1,2},{2,1},{3,0},{4,7},{5,6},{6,5},{7,4},{8,11},{9,10},{10,... | collective-permute-start | bytes 1966088 | tf_op jit(solution)/shard_map/ppermute | solution.py:23
  44.1 30.3 %collective-permute-start.18 = (bf16[1024,256]{1,0:T(8,128)(2,1)S(1)}, bf16[1024,256]{1,0:T(8,128)(2,1)S(1)}, u32[]{:S(2)}, u32[]{:S(2)}) collective-permute-start(bf16[1024,256]{1,0:T(8,128)(2,1)S(1)} %constant_dynamic-update-slice_fusion.5), channel_id=1, source_target_pairs={{0,1},{1,0},{2,3},{3,2},{4,5},{5,4},{6,7},{7,6},{8,9},{9,8},{10,11... | collective-permute-start | bytes 1572872 | tf_op jit(solution)/shard_map/ppermute | solution.py:23
  48.0 26.9 %collective-permute-start.13 = (bf16[1024,256]{1,0:T(8,128)(2,1)S(1)}, bf16[1024,256]{1,0:T(8,128)(2,1)}, u32[]{:S(2)}, u32[]{:S(2)}) collective-permute-start(bf16[1024,256]{1,0:T(8,128)(2,1)S(1)} %constant_dynamic-update-slice_fusion.5), channel_id=1, source_target_pairs={{0,12},{4,8},{8,4},{12,0},{16,28},{20,24},{24,20},{28,16},{32,44},... | collective-permute-start | bytes 1572872 | tf_op jit(solution)/shard_map/ppermute | solution.py:23
  49.8 25.4 %collective-permute-start.12 = (bf16[1024,256]{1,0:T(8,128)(2,1)S(1)}, bf16[1024,256]{1,0:T(8,128)(2,1)}, u32[]{:S(2)}, u32[]{:S(2)}) collective-permute-start(bf16[1024,256]{1,0:T(8,128)(2,1)S(1)} %constant_dynamic-update-slice_fusion.5), channel_id=1, source_target_pairs={{0,8},{4,12},{8,0},{12,4},{16,24},{20,28},{24,16},{28,20},{32,40},... | collective-permute-start | bytes 1572872 | tf_op jit(solution)/shard_map/ppermute | solution.py:23
  50.5 27.2 %collective-permute-start.11 = (bf16[1024,256]{1,0:T(8,128)(2,1)S(1)}, bf16[1024,256]{1,0:T(8,128)(2,1)}, u32[]{:S(2)}, u32[]{:S(2)}) collective-permute-start(bf16[1024,256]{1,0:T(8,128)(2,1)S(1)} %constant_dynamic-update-slice_fusion.5), channel_id=1, source_target_pairs={{0,4},{4,0},{8,12},{12,8},{16,20},{20,16},{24,28},{28,24},{32,36},... | collective-permute-start | bytes 1572872 | tf_op jit(solution)/shard_map/ppermute | solution.py:23
  56.8 23.7 %collective-permute-start.14 = (bf16[1024,256]{1,0:T(8,128)(2,1)}, bf16[1024,256]{1,0:T(8,128)(2,1)}, u32[]{:S(2)}, u32[]{:S(2)}) collective-permute-start(bf16[1024,256]{1,0:T(8,128)(2,1)} %constant_dynamic-update-slice_fusion), channel_id=1, source_target_pairs={{0,1},{1,0},{2,3},{3,2},{4,5},{5,4},{6,7},{7,6},{8,9},{9,8},{10,11... | collective-permute-start | bytes 1572872 | tf_op jit(solution)/shard_map/ppermute | solution.py:23
  74.4 26.3 %collective-permute-start.7 = (bf16[1024,256]{1,0:T(8,128)(2,1)}, bf16[1024,256]{1,0:T(8,128)(2,1)S(1)}, u32[]{:S(2)}, u32[]{:S(2)}) collective-permute-start(bf16[1024,256]{1,0:T(8,128)(2,1)} %constant_dynamic-update-slice_fusion), channel_id=1, source_target_pairs={{0,96},{4,100},{8,104},{12,108},{16,112},{20,116},{24,120},{28,124... | collective-permute-start | bytes 1572872 | tf_op jit(solution)/shard_map/ppermute | solution.py:23
  74.9 26.6 %collective-permute-start.6 = (bf16[1024,256]{1,0:T(8,128)(2,1)}, bf16[1024,256]{1,0:T(8,128)(2,1)S(1)}, u32[]{:S(2)}, u32[]{:S(2)}) collective-permute-start(bf16[1024,256]{1,0:T(8,128)(2,1)} %constant_dynamic-update-slice_fusion), channel_id=1, source_target_pairs={{0,64},{4,68},{8,72},{12,76},{16,80},{20,84},{24,88},{28,92},{32,9... | collective-permute-start | bytes 1572872 | tf_op jit(solution)/shard_map/ppermute | solution.py:23
  75.2 26.6 %collective-permute-start.5 = (bf16[1024,256]{1,0:T(8,128)(2,1)}, bf16[1024,256]{1,0:T(8,128)(2,1)S(1)}, u32[]{:S(2)}, u32[]{:S(2)}) collective-permute-start(bf16[1024,256]{1,0:T(8,128)(2,1)} %constant_dynamic-update-slice_fusion), channel_id=1, source_target_pairs={{0,32},{4,36},{8,40},{12,44},{16,48},{20,52},{24,56},{28,60},{32,0... | collective-permute-start | bytes 1572872 | tf_op jit(solution)/shard_map/ppermute | solution.py:23
  77.7 24.6 %collective-permute-start.21 = (bf16[1024,256]{1,0:T(8,128)(2,1)}, bf16[1024,256]{1,0:T(8,128)(2,1)S(1)}, u32[]{:S(2)}, u32[]{:S(2)}) collective-permute-start(bf16[1024,256]{1,0:T(8,128)(2,1)} %collective-permute-done.13), channel_id=1, source_target_pairs={{0,1},{1,0},{2,3},{3,2},{4,5},{5,4},{6,7},{7,6},{8,9},{9,8},{10,11... | collective-permute-start | bytes 1572872 | tf_op jit(solution)/shard_map/ppermute | solution.py:23
  80.5 22.9 %collective-permute-start.20 = (bf16[1024,256]{1,0:T(8,128)(2,1)}, bf16[1024,256]{1,0:T(8,128)(2,1)S(1)}, u32[]{:S(2)}, u32[]{:S(2)}) collective-permute-start(bf16[1024,256]{1,0:T(8,128)(2,1)} %collective-permute-done.12), channel_id=1, source_target_pairs={{0,1},{1,0},{2,3},{3,2},{4,5},{5,4},{6,7},{7,6},{8,9},{9,8},{10,11... | collective-permute-start | bytes 1572872 | tf_op jit(solution)/shard_map/ppermute | solution.py:23
  104.7 55.3 %collective-permute-start.34 = (bf16[64,64]{1,0:T(8,128)(2,1)S(1)}, bf16[64,64]{1,0:T(8,128)(2,1)S(1)}, u32[]{:S(2)}, u32[]{:S(2)}) collective-permute-start(bf16[64,64]{1,0:T(8,128)(2,1)S(1)} %copy-done.155), channel_id=1, source_target_pairs={{0,3},{1,2},{2,1},{3,0},{4,7},{5,6},{6,5},{7,4},{8,11},{9,10},{10,... | collective-permute-start | bytes 24584 | tf_op jit(solution)/shard_map/ppermute | solution.py:23
  104.9 57.8 %collective-permute-start.32 = (bf16[64,64]{1,0:T(8,128)(2,1)S(1)}, bf16[64,64]{1,0:T(8,128)(2,1)S(1)}, u32[]{:S(2)}, u32[]{:S(2)}) collective-permute-start(bf16[64,64]{1,0:T(8,128)(2,1)S(1)} %copy-done.154), channel_id=1, source_target_pairs={{0,1},{1,0},{2,3},{3,2},{4,5},{5,4},{6,7},{7,6},{8,9},{9,8},{10,11... | collective-permute-start | bytes 24584 | tf_op jit(solution)/shard_map/ppermute | solution.py:23
  105.3 57.4 %collective-permute-start.33 = (bf16[64,64]{1,0:T(8,128)(2,1)S(1)}, bf16[64,64]{1,0:T(8,128)(2,1)S(1)}, u32[]{:S(2)}, u32[]{:S(2)}) collective-permute-start(bf16[64,64]{1,0:T(8,128)(2,1)S(1)} %copy-done.153), channel_id=1, source_target_pairs={{0,2},{1,3},{2,0},{3,1},{4,6},{5,7},{6,4},{7,5},{8,10},{9,11},{10,... | collective-permute-start | bytes 24584 | tf_op jit(solution)/shard_map/ppermute | solution.py:23
  151.5 36.2 %collective-permute-start.116 = (bf16[256,2048]{1,0:T(8,128)(2,1)}, bf16[256,2048]{1,0:T(8,128)(2,1)}, u32[]{:S(2)}, u32[]{:S(2)}) collective-permute-start(bf16[256,2048]{1,0:T(8,128)(2,1)} %pad_maximum_fusion), channel_id=1, source_target_pairs={{0,4},{4,0},{8,12},{12,8},{16,20},{20,16},{24,28},{28,24},{32,36},... | collective-permute-start | bytes 3145736 | tf_op jit(solution)/shard_map/ppermute | solution.py:23
  158.4 47.8 %collective-permute-start.118 = (bf16[256,2048]{1,0:T(8,128)(2,1)}, bf16[256,2048]{1,0:T(8,128)(2,1)}, u32[]{:S(2)}, u32[]{:S(2)}) collective-permute-start(bf16[256,2048]{1,0:T(8,128)(2,1)} %pad_maximum_fusion), channel_id=1, source_target_pairs={{0,12},{4,8},{8,4},{12,0},{16,28},{20,24},{24,20},{28,16},{32,44},... | collective-permute-start | bytes 3145736 | tf_op jit(solution)/shard_map/ppermute | solution.py:23
  160.0 39.3 %collective-permute-start.117 = (bf16[256,2048]{1,0:T(8,128)(2,1)}, bf16[256,2048]{1,0:T(8,128)(2,1)}, u32[]{:S(2)}, u32[]{:S(2)}) collective-permute-start(bf16[256,2048]{1,0:T(8,128)(2,1)} %pad_maximum_fusion), channel_id=1, source_target_pairs={{0,8},{4,12},{8,0},{12,4},{16,24},{20,28},{24,16},{28,20},{32,40},... | collective-permute-start | bytes 3145736 | tf_op jit(solution)/shard_map/ppermute | solution.py:23
  183.0 72.9 %collective-permute-start.144 = (bf16[256,2048]{1,0:T(8,128)(2,1)}, bf16[256,2048]{1,0:T(8,128)(2,1)}, u32[]{:S(2)}, u32[]{:S(2)}) collective-permute-start(bf16[256,2048]{1,0:T(8,128)(2,1)} %get-tuple-element.366), channel_id=1, source_target_pairs={{0,96},{4,100},{8,104},{12,108},{16,112},{20,116},{24,120},{28,124... | collective-permute-start | bytes 3145736 | tf_op jit(solution)/shard_map/ppermute | solution.py:23
  184.9 15.8 %collective-permute-start.38 = (bf16[64,2048]{1,0:T(8,128)(2,1)}, bf16[64,2048]{1,0:T(8,128)(2,1)}, u32[]{:S(2)}, u32[]{:S(2)}) collective-permute-start(bf16[64,2048]{1,0:T(8,128)(2,1)} %multiply_convert_fusion.5), channel_id=1, source_target_pairs={{0,2},{1,3},{2,0},{3,1},{4,6},{5,7},{6,4},{7,5},{8,10},{9,11},{10,... | collective-permute-start | bytes 786440 | tf_op jit(solution)/shard_map/ppermute | solution.py:23
  187.7 22.5 %collective-permute-start.39 = (bf16[64,2048]{1,0:T(8,128)(2,1)}, bf16[64,2048]{1,0:T(8,128)(2,1)S(1)}, u32[]{:S(2)}, u32[]{:S(2)}) collective-permute-start(bf16[64,2048]{1,0:T(8,128)(2,1)} %multiply_convert_fusion.5), channel_id=1, source_target_pairs={{0,1},{1,0},{2,3},{3,2},{4,5},{5,4},{6,7},{7,6},{8,9},{9,8},{10,11... | collective-permute-start | bytes 786440 | tf_op jit(solution)/shard_map/ppermute | solution.py:23
  206.2 23.1 %collective-permute-start.35 = (bf16[64,2048]{1,0:T(8,128)(2,1)S(1)}, bf16[64,2048]{1,0:T(8,128)(2,1)S(1)}, u32[]{:S(2)}, u32[]{:S(2)}) collective-permute-start(bf16[64,2048]{1,0:T(8,128)(2,1)S(1)} %copy-done.105), channel_id=1, source_target_pairs={{0,1},{1,0},{2,3},{3,2},{4,5},{5,4},{6,7},{7,6},{8,9},{9,8},{10,11... | collective-permute-start | bytes 786440 | tf_op jit(solution)/shard_map/ppermute | solution.py:23
  210.2 19.2 %collective-permute-start.37 = (bf16[64,2048]{1,0:T(8,128)(2,1)S(1)}, bf16[64,2048]{1,0:T(8,128)(2,1)S(1)}, u32[]{:S(2)}, u32[]{:S(2)}) collective-permute-start(bf16[64,2048]{1,0:T(8,128)(2,1)S(1)} %collective-permute-done.36), channel_id=1, source_target_pairs={{0,1},{1,0},{2,3},{3,2},{4,5},{5,4},{6,7},{7,6},{8,9},{9,8},{10,11... | collective-permute-start | bytes 786440 | tf_op jit(solution)/shard_map/ppermute | solution.py:23
  221.3 19.3 %collective-permute-start.121 = (bf16[256,512]{1,0:T(8,128)(2,1)S(1)}, bf16[256,512]{1,0:T(8,128)(2,1)S(1)}, u32[]{:S(2)}, u32[]{:S(2)}) collective-permute-start(bf16[256,512]{1,0:T(8,128)(2,1)S(1)} %get-tuple-element.223), channel_id=1, source_target_pairs={{0,12},{4,8},{8,4},{12,0},{16,28},{20,24},{24,20},{28,16},{32,44},... | collective-permute-start | bytes 786440 | tf_op jit(solution)/shard_map/ppermute | solution.py:23
  232.9 25.8 %collective-permute-start.143 = (bf16[256,2048]{1,0:T(8,128)(2,1)}, bf16[256,2048]{1,0:T(8,128)(2,1)S(1)}, u32[]{:S(2)}, u32[]{:S(2)}) collective-permute-start(bf16[256,2048]{1,0:T(8,128)(2,1)} %get-tuple-element.366), channel_id=1, source_target_pairs={{0,64},{4,68},{8,72},{12,76},{16,80},{20,84},{24,88},{28,92},{32,9... | collective-permute-start | bytes 3145736 | tf_op jit(solution)/shard_map/ppermute | solution.py:23
  240.6 39.4 %collective-permute-start.142 = (bf16[256,2048]{1,0:T(8,128)(2,1)}, bf16[256,2048]{1,0:T(8,128)(2,1)S(1)}, u32[]{:S(2)}, u32[]{:S(2)}) collective-permute-start(bf16[256,2048]{1,0:T(8,128)(2,1)} %get-tuple-element.366), channel_id=1, source_target_pairs={{0,32},{4,36},{8,40},{12,44},{16,48},{20,52},{24,56},{28,60},{32,0... | collective-permute-start | bytes 3145736 | tf_op jit(solution)/shard_map/ppermute | solution.py:23
  248.8 37.2 %collective-permute-start.140 = (bf16[256,512]{1,0:T(8,128)(2,1)S(1)}, bf16[256,512]{1,0:T(8,128)(2,1)S(1)}, u32[]{:S(2)}, u32[]{:S(2)}) collective-permute-start(bf16[256,512]{1,0:T(8,128)(2,1)S(1)} %get-tuple-element.215), channel_id=1, source_target_pairs={{0,64},{4,68},{8,72},{12,76},{16,80},{20,84},{24,88},{28,92},{32,9... | collective-permute-start | bytes 786440 | tf_op jit(solution)/shard_map/ppermute | solution.py:23
  251.9 39.3 %collective-permute-start.139 = (bf16[256,512]{1,0:T(8,128)(2,1)S(1)}, bf16[256,512]{1,0:T(8,128)(2,1)S(1)}, u32[]{:S(2)}, u32[]{:S(2)}) collective-permute-start(bf16[256,512]{1,0:T(8,128)(2,1)S(1)} %get-tuple-element.216), channel_id=1, source_target_pairs={{0,32},{4,36},{8,40},{12,44},{16,48},{20,52},{24,56},{28,60},{32,0... | collective-permute-start | bytes 786440 | tf_op jit(solution)/shard_map/ppermute | solution.py:23
  255.9 36.5 %collective-permute-start.141 = (bf16[256,512]{1,0:T(8,128)(2,1)S(1)}, bf16[256,512]{1,0:T(8,128)(2,1)S(1)}, u32[]{:S(2)}, u32[]{:S(2)}) collective-permute-start(bf16[256,512]{1,0:T(8,128)(2,1)S(1)} %get-tuple-element.217), channel_id=1, source_target_pairs={{0,96},{4,100},{8,104},{12,108},{16,112},{20,116},{24,120},{28,124... | collective-permute-start | bytes 786440 | tf_op jit(solution)/shard_map/ppermute | solution.py:23
  258.7 37.7 %collective-permute-start.41 = (bf16[128,2048]{1,0:T(8,128)(2,1)S(1)}, bf16[128,2048]{1,0:T(8,128)(2,1)S(1)}, u32[]{:S(2)}, u32[]{:S(2)}) collective-permute-start(bf16[128,2048]{1,0:T(8,128)(2,1)S(1)} %slice.694), channel_id=1, source_target_pairs={{0,1},{1,0},{2,3},{3,2},{4,5},{5,4},{6,7},{7,6},{8,9},{9,8},{10,11... | collective-permute-start | bytes 1572872 | tf_op jit(solution)/shard_map/ppermute | solution.py:23
  280.0 27.2 %collective-permute-start.122 = (bf16[2,4,64,512]{3,2,1,0:T(8,128)(2,1)S(1)}, bf16[2,4,64,512]{3,2,1,0:T(8,128)(2,1)S(1)}, u32[]{:S(2)}, u32[]{:S(2)}) collective-permute-start(bf16[2,4,64,512]{3,2,1,0:T(8,128)(2,1)S(1)} %get-tuple-element.194), channel_id=1, source_target_pairs={{0,32},{4,36},{8,40},{12,44},{16,48},{20,52},{24,56},{28,60},{32,0... | collective-permute-start | bytes 1572872 | tf_op jit(solution)/shard_map/ppermute | solution.py:23
  286.0 23.0 %collective-permute-start.124 = (bf16[2,4,64,512]{3,2,1,0:T(8,128)(2,1)S(1)}, bf16[2,4,64,512]{3,2,1,0:T(8,128)(2,1)S(1)}, u32[]{:S(2)}, u32[]{:S(2)}) collective-permute-start(bf16[2,4,64,512]{3,2,1,0:T(8,128)(2,1)S(1)} %get-tuple-element.195), channel_id=1, source_target_pairs={{0,96},{4,100},{8,104},{12,108},{16,112},{20,116},{24,120},{28,124... | collective-permute-start | bytes 1572872 | tf_op jit(solution)/shard_map/ppermute | solution.py:23
  291.3 22.8 %collective-permute-start.123 = (bf16[2,4,64,512]{3,2,1,0:T(8,128)(2,1)S(1)}, bf16[2,4,64,512]{3,2,1,0:T(8,128)(2,1)S(1)}, u32[]{:S(2)}, u32[]{:S(2)}) collective-permute-start(bf16[2,4,64,512]{3,2,1,0:T(8,128)(2,1)S(1)} %get-tuple-element.196), channel_id=1, source_target_pairs={{0,64},{4,68},{8,72},{12,76},{16,80},{20,84},{24,88},{28,92},{32,9... | collective-permute-start | bytes 1572872 | tf_op jit(solution)/shard_map/ppermute | solution.py:23
  292.4 32.6 %collective-permute-start.132 = (bf16[2,4,64,512]{3,2,1,0:T(8,128)(2,1)S(1)}, bf16[2,4,64,512]{3,2,1,0:T(8,128)(2,1)S(1)}, u32[]{:S(2)}, u32[]{:S(2)}) collective-permute-start(bf16[2,4,64,512]{3,2,1,0:T(8,128)(2,1)S(1)} %get-tuple-element.191), channel_id=1, source_target_pairs={{0,32},{4,36},{8,40},{12,44},{16,48},{20,52},{24,56},{28,60},{32,0... | collective-permute-start | bytes 1572872 | tf_op jit(solution)/shard_map/ppermute | solution.py:23
  302.2 25.2 %collective-permute-start.134 = (bf16[2,4,64,512]{3,2,1,0:T(8,128)(2,1)S(1)}, bf16[2,4,64,512]{3,2,1,0:T(8,128)(2,1)S(1)}, u32[]{:S(2)}, u32[]{:S(2)}) collective-permute-start(bf16[2,4,64,512]{3,2,1,0:T(8,128)(2,1)S(1)} %get-tuple-element.192), channel_id=1, source_target_pairs={{0,96},{4,100},{8,104},{12,108},{16,112},{20,116},{24,120},{28,124... | collective-permute-start | bytes 1572872 | tf_op jit(solution)/shard_map/ppermute | solution.py:23
  307.3 29.3 %collective-permute-start.133 = (bf16[2,4,64,512]{3,2,1,0:T(8,128)(2,1)S(1)}, bf16[2,4,64,512]{3,2,1,0:T(8,128)(2,1)S(1)}, u32[]{:S(2)}, u32[]{:S(2)}) collective-permute-start(bf16[2,4,64,512]{3,2,1,0:T(8,128)(2,1)S(1)} %get-tuple-element.193), channel_id=1, source_target_pairs={{0,64},{4,68},{8,72},{12,76},{16,80},{20,84},{24,88},{28,92},{32,9... | collective-permute-start | bytes 1572872 | tf_op jit(solution)/shard_map/ppermute | solution.py:23
  308.9 34.5 %collective-permute-start.145 = (bf16[2,64,2048]{2,1,0:T(8,128)(2,1)S(1)}, bf16[2,64,2048]{2,1,0:T(8,128)(2,1)S(1)}, u32[]{:S(2)}, u32[]{:S(2)}) collective-permute-start(bf16[2,64,2048]{2,1,0:T(8,128)(2,1)S(1)} %get-tuple-element.188), channel_id=1, source_target_pairs={{0,4},{4,0},{8,12},{12,8},{16,20},{20,16},{24,28},{28,24},{32,36},... | collective-permute-start | bytes 1572872 | tf_op jit(solution)/shard_map/ppermute | solution.py:23
  314.1 36.1 %collective-permute-start.147 = (bf16[2,64,2048]{2,1,0:T(8,128)(2,1)S(1)}, bf16[2,64,2048]{2,1,0:T(8,128)(2,1)S(1)}, u32[]{:S(2)}, u32[]{:S(2)}) collective-permute-start(bf16[2,64,2048]{2,1,0:T(8,128)(2,1)S(1)} %get-tuple-element.189), channel_id=1, source_target_pairs={{0,12},{4,8},{8,4},{12,0},{16,28},{20,24},{24,20},{28,16},{32,44},... | collective-permute-start | bytes 1572872 | tf_op jit(solution)/shard_map/ppermute | solution.py:23
  325.0 25.3 %collective-permute-start.146 = (bf16[2,64,2048]{2,1,0:T(8,128)(2,1)S(1)}, bf16[2,64,2048]{2,1,0:T(8,128)(2,1)S(1)}, u32[]{:S(2)}, u32[]{:S(2)}) collective-permute-start(bf16[2,64,2048]{2,1,0:T(8,128)(2,1)S(1)} %get-tuple-element.190), channel_id=1, source_target_pairs={{0,8},{4,12},{8,0},{12,4},{16,24},{20,28},{24,16},{28,20},{32,40},... | collective-permute-start | bytes 1572872 | tf_op jit(solution)/shard_map/ppermute | solution.py:23
  327.4 77.8 %collective-permute-start.44 = (bf16[64,2048]{1,0:T(8,128)(2,1)}, bf16[64,2048]{1,0:T(8,128)(2,1)}, u32[]{:S(2)}, u32[]{:S(2)}) collective-permute-start(bf16[64,2048]{1,0:T(8,128)(2,1)} %multiply_convert_fusion.4), channel_id=1, source_target_pairs={{0,1},{1,0},{2,3},{3,2},{4,5},{5,4},{6,7},{7,6},{8,9},{9,8},{10,11... | collective-permute-start | bytes 786440 | tf_op jit(solution)/shard_map/ppermute | solution.py:23
  336.6 59.0 %collective-permute-start.43 = (bf16[64,2048]{1,0:T(8,128)(2,1)}, bf16[64,2048]{1,0:T(8,128)(2,1)}, u32[]{:S(2)}, u32[]{:S(2)}) collective-permute-start(bf16[64,2048]{1,0:T(8,128)(2,1)} %multiply_convert_fusion.4), channel_id=1, source_target_pairs={{0,2},{1,3},{2,0},{3,1},{4,6},{5,7},{6,4},{7,5},{8,10},{9,11},{10,... | collective-permute-start | bytes 786440 | tf_op jit(solution)/shard_map/ppermute | solution.py:23
  343.4 44.7 %collective-permute-start.125 = (bf16[4,64,512]{2,1,0:T(8,128)(2,1)}, bf16[4,64,512]{2,1,0:T(8,128)(2,1)}, u32[]{:S(2)}, u32[]{:S(2)}) collective-permute-start(bf16[4,64,512]{2,1,0:T(8,128)(2,1)} %dynamic-slice_bitcast_fusion.14), channel_id=1, source_target_pairs={{0,16},{4,20},{8,24},{12,28},{16,0},{20,4},{24,8},{28,12},{32,48},... | collective-permute-start | bytes 786440 | tf_op jit(solution)/shard_map/ppermute | solution.py:23
  350.2 42.7 %collective-permute-start.135 = (bf16[4,64,512]{2,1,0:T(8,128)(2,1)}, bf16[4,64,512]{2,1,0:T(8,128)(2,1)}, u32[]{:S(2)}, u32[]{:S(2)}) collective-permute-start(bf16[4,64,512]{2,1,0:T(8,128)(2,1)} %dynamic-slice_bitcast_fusion.13), channel_id=1, source_target_pairs={{0,16},{4,20},{8,24},{12,28},{16,0},{20,4},{24,8},{28,12},{32,48},... | collective-permute-start | bytes 786440 | tf_op jit(solution)/shard_map/ppermute | solution.py:23
  351.5 39.1 %collective-permute-start.148 = (bf16[64,2048]{1,0:T(8,128)(2,1)}, bf16[64,2048]{1,0:T(8,128)(2,1)}, u32[]{:S(2)}, u32[]{:S(2)}) collective-permute-start(bf16[64,2048]{1,0:T(8,128)(2,1)} %dynamic-slice_bitcast_fusion.12), channel_id=1, source_target_pairs={{0,16},{4,20},{8,24},{12,28},{16,0},{20,4},{24,8},{28,12},{32,48},... | collective-permute-start | bytes 786440 | tf_op jit(solution)/shard_map/ppermute | solution.py:23
  403.8 63.2 %collective-permute-start.107 = (bf16[336,2048]{1,0:T(8,128)(2,1)}, bf16[336,2048]{1,0:T(8,128)(2,1)}, u32[]{:S(2)}, u32[]{:S(2)}) collective-permute-start(bf16[336,2048]{1,0:T(8,128)(2,1)} %concatenate.166), channel_id=1, source_target_pairs={{0,1},{1,0},{2,3},{3,2},{4,5},{5,4},{6,7},{7,6},{8,9},{9,8},{10,11... | collective-permute-start | bytes 4128776 | tf_op jit(solution)/shard_map/ppermute | solution.py:23
  410.6 32.0 %collective-permute-start.100 = (bf16[2,4,64,512]{3,2,0,1:T(8,128)(2,1)}, bf16[2,4,64,512]{3,2,0,1:T(8,128)(2,1)}, u32[]{:S(2)}, u32[]{:S(2)}) collective-permute-start(bf16[2,4,64,512]{3,2,0,1:T(8,128)(2,1)} %bitcast.340), channel_id=1, source_target_pairs={{0,32},{4,36},{8,40},{12,44},{16,48},{20,52},{24,56},{28,60},{32,0... | collective-permute-start | bytes 1572872 | tf_op jit(solution)/shard_map/ppermute | solution.py:23
  410.6 32.1 %collective-permute-start.101 = (bf16[2,4,64,512]{3,2,0,1:T(8,128)(2,1)}, bf16[2,4,64,512]{3,2,0,1:T(8,128)(2,1)}, u32[]{:S(2)}, u32[]{:S(2)}) collective-permute-start(bf16[2,4,64,512]{3,2,0,1:T(8,128)(2,1)} %bitcast.339), channel_id=1, source_target_pairs={{0,64},{4,68},{8,72},{12,76},{16,80},{20,84},{24,88},{28,92},{32,9... | collective-permute-start | bytes 1572872 | tf_op jit(solution)/shard_map/ppermute | solution.py:23
  410.7 32.5 %collective-permute-start.102 = (bf16[2,4,64,512]{3,2,0,1:T(8,128)(2,1)}, bf16[2,4,64,512]{3,2,0,1:T(8,128)(2,1)}, u32[]{:S(2)}, u32[]{:S(2)}) collective-permute-start(bf16[2,4,64,512]{3,2,0,1:T(8,128)(2,1)} %bitcast.338), channel_id=1, source_target_pairs={{0,96},{4,100},{8,104},{12,108},{16,112},{20,116},{24,120},{28,124... | collective-permute-start | bytes 1572872 | tf_op jit(solution)/shard_map/ppermute | solution.py:23
  453.3 20.4 %collective-permute-start.46 = (bf16[8,128,256]{2,1,0:T(8,128)(2,1)S(1)}, bf16[8,128,256]{2,1,0:T(8,128)(2,1)S(1)}, u32[]{:S(2)}, u32[]{:S(2)}) collective-permute-start(bf16[8,128,256]{2,1,0:T(8,128)(2,1)S(1)} %copy-done.40), channel_id=1, source_target_pairs={{0,1},{1,0},{2,3},{3,2},{4,5},{5,4},{6,7},{7,6},{8,9},{9,8},{10,11... | collective-permute-start | bytes 1572872 | tf_op jit(solution)/shard_map/ppermute | solution.py:23
  458.9 35.4 %collective-permute-start.57 = (bf16[8,128,256]{2,1,0:T(8,128)(2,1)S(1)}, bf16[8,128,256]{2,1,0:T(8,128)(2,1)S(1)}, u32[]{:S(2)}, u32[]{:S(2)}) collective-permute-start(bf16[8,128,256]{2,1,0:T(8,128)(2,1)S(1)} %copy-done.38), channel_id=1, source_target_pairs={{0,1},{1,0},{2,3},{3,2},{4,5},{5,4},{6,7},{7,6},{8,9},{9,8},{10,11... | collective-permute-start | bytes 1572872 | tf_op jit(solution)/shard_map/ppermute | solution.py:23
  466.4 17.2 %collective-permute-start.50 = (bf16[8,128,256]{2,1,0:T(8,128)(2,1)S(1)}, bf16[8,128,256]{2,1,0:T(8,128)(2,1)S(1)}, u32[]{:S(2)}, u32[]{:S(2)}) collective-permute-start(bf16[8,128,256]{2,1,0:T(8,128)(2,1)S(1)} %add_convert_fusion.4), channel_id=1, source_target_pairs={{0,64},{4,68},{8,72},{12,76},{16,80},{20,84},{24,88},{28,92},{32,9... | collective-permute-start | bytes 1572872 | tf_op jit(solution)/shard_map/ppermute | solution.py:23
  467.1 26.1 %collective-permute-start.52 = (bf16[8,128,256]{2,1,0:T(8,128)(2,1)S(1)}, bf16[8,128,256]{2,1,0:T(8,128)(2,1)S(1)}, u32[]{:S(2)}, u32[]{:S(2)}) collective-permute-start(bf16[8,128,256]{2,1,0:T(8,128)(2,1)S(1)} %add_convert_fusion.3), channel_id=1, source_target_pairs={{0,96},{4,100},{8,104},{12,108},{16,112},{20,116},{24,120},{28,124... | collective-permute-start | bytes 1572872 | tf_op jit(solution)/shard_map/ppermute | solution.py:23
  473.7 21.1 %collective-permute-start.59 = (bf16[8,128,256]{2,1,0:T(8,128)(2,1)S(1)}, bf16[8,128,256]{2,1,0:T(8,128)(2,1)S(1)}, u32[]{:S(2)}, u32[]{:S(2)}) collective-permute-start(bf16[8,128,256]{2,1,0:T(8,128)(2,1)S(1)} %add_convert_fusion.2), channel_id=1, source_target_pairs={{0,4},{4,0},{8,12},{12,8},{16,20},{20,16},{24,28},{28,24},{32,36},... | collective-permute-start | bytes 1572872 | tf_op jit(solution)/shard_map/ppermute | solution.py:23
  473.9 21.9 %collective-permute-start.61 = (bf16[8,128,256]{2,1,0:T(8,128)(2,1)S(1)}, bf16[8,128,256]{2,1,0:T(8,128)(2,1)S(1)}, u32[]{:S(2)}, u32[]{:S(2)}) collective-permute-start(bf16[8,128,256]{2,1,0:T(8,128)(2,1)S(1)} %add_convert_fusion.1), channel_id=1, source_target_pairs={{0,8},{4,12},{8,0},{12,4},{16,24},{20,28},{24,16},{28,20},{32,40},... | collective-permute-start | bytes 1572872 | tf_op jit(solution)/shard_map/ppermute | solution.py:23
  483.5 28.2 %collective-permute-start.63 = (bf16[8,128,256]{2,1,0:T(8,128)(2,1)S(1)}, bf16[8,128,256]{2,1,0:T(8,128)(2,1)S(1)}, u32[]{:S(2)}, u32[]{:S(2)}) collective-permute-start(bf16[8,128,256]{2,1,0:T(8,128)(2,1)S(1)} %add_convert_fusion), channel_id=1, source_target_pairs={{0,12},{4,8},{8,4},{12,0},{16,28},{20,24},{24,20},{28,16},{32,44},... | collective-permute-start | bytes 1572872 | tf_op jit(solution)/shard_map/ppermute | solution.py:23
  493.2 58.7 %collective-permute-start.108 = (bf16[168,2048]{1,0:T(8,128)(2,1)}, bf16[168,2048]{1,0:T(8,128)(2,1)}, u32[]{:S(2)}, u32[]{:S(2)}) collective-permute-start(bf16[168,2048]{1,0:T(8,128)(2,1)} %slice.692), channel_id=1, source_target_pairs={{0,2},{1,3},{2,0},{3,1},{4,6},{5,7},{6,4},{7,5},{8,10},{9,11},{10,... | collective-permute-start | bytes 2064392 | tf_op jit(solution)/shard_map/ppermute | solution.py:23
  494.3 18.4 %collective-permute-start.53 = (bf16[2,128,256]{2,1,0:T(8,128)(2,1)S(1)}, bf16[2,128,256]{2,1,0:T(8,128)(2,1)S(1)}, u32[]{:S(2)}, u32[]{:S(2)}) collective-permute-start(bf16[2,128,256]{2,1,0:T(8,128)(2,1)S(1)} %get-tuple-element.276), channel_id=1, source_target_pairs={{0,4},{4,0},{8,12},{12,8},{16,20},{20,16},{24,28},{28,24},{32,36},... | collective-permute-start | bytes 393224 | tf_op jit(solution)/shard_map/ppermute | solution.py:23
  494.8 19.8 %collective-permute-start.55 = (bf16[2,128,256]{2,1,0:T(8,128)(2,1)S(1)}, bf16[2,128,256]{2,1,0:T(8,128)(2,1)S(1)}, u32[]{:S(2)}, u32[]{:S(2)}) collective-permute-start(bf16[2,128,256]{2,1,0:T(8,128)(2,1)S(1)} %get-tuple-element.277), channel_id=1, source_target_pairs={{0,12},{4,8},{8,4},{12,0},{16,28},{20,24},{24,20},{28,16},{32,44},... | collective-permute-start | bytes 393224 | tf_op jit(solution)/shard_map/ppermute | solution.py:23
  495.8 20.6 %collective-permute-start.54 = (bf16[2,128,256]{2,1,0:T(8,128)(2,1)S(1)}, bf16[2,128,256]{2,1,0:T(8,128)(2,1)S(1)}, u32[]{:S(2)}, u32[]{:S(2)}) collective-permute-start(bf16[2,128,256]{2,1,0:T(8,128)(2,1)S(1)} %get-tuple-element.278), channel_id=1, source_target_pairs={{0,8},{4,12},{8,0},{12,4},{16,24},{20,28},{24,16},{28,20},{32,40},... | collective-permute-start | bytes 393224 | tf_op jit(solution)/shard_map/ppermute | solution.py:23
  539.6 72.0 %collective-permute-start.86 = (bf16[4,2,64,512]{3,2,1,0:T(8,128)(2,1)}, bf16[4,2,64,512]{3,2,1,0:T(8,128)(2,1)}, u32[]{:S(2)}, u32[]{:S(2)}) collective-permute-start(bf16[4,2,64,512]{3,2,1,0:T(8,128)(2,1)} %get-tuple-element.205), channel_id=1, source_target_pairs={{0,4},{4,0},{8,12},{12,8},{16,20},{20,16},{24,28},{28,24},{32,36},... | collective-permute-start | bytes 1572872 | tf_op jit(solution)/shard_map/ppermute | solution.py:23
  539.6 72.0 %collective-permute-start.88 = (bf16[4,2,64,512]{3,2,1,0:T(8,128)(2,1)}, bf16[4,2,64,512]{3,2,1,0:T(8,128)(2,1)}, u32[]{:S(2)}, u32[]{:S(2)}) collective-permute-start(bf16[4,2,64,512]{3,2,1,0:T(8,128)(2,1)} %get-tuple-element.206), channel_id=1, source_target_pairs={{0,12},{4,8},{8,4},{12,0},{16,28},{20,24},{24,20},{28,16},{32,44},... | collective-permute-start | bytes 1572872 | tf_op jit(solution)/shard_map/ppermute | solution.py:23
  577.8 33.8 %collective-permute-start.87 = (bf16[4,2,64,512]{3,2,1,0:T(8,128)(2,1)S(1)}, bf16[4,2,64,512]{3,2,1,0:T(8,128)(2,1)S(1)}, u32[]{:S(2)}, u32[]{:S(2)}) collective-permute-start(bf16[4,2,64,512]{3,2,1,0:T(8,128)(2,1)S(1)} %copy-done.107), channel_id=1, source_target_pairs={{0,8},{4,12},{8,0},{12,4},{16,24},{20,28},{24,16},{28,20},{32,40},... | collective-permute-start | bytes 1572872 | tf_op jit(solution)/shard_map/ppermute | solution.py:23
  587.8 22.0 %collective-permute-start.113 = (bf16[2,64,168]{2,1,0:T(8,128)(2,1)S(1)}, bf16[2,64,168]{2,1,0:T(8,128)(2,1)S(1)}, u32[]{:S(2)}, u32[]{:S(2)}) collective-permute-start(bf16[2,64,168]{2,1,0:T(8,128)(2,1)S(1)} %get-tuple-element.306), channel_id=1, source_target_pairs={{0,64},{4,68},{8,72},{12,76},{16,80},{20,84},{24,88},{28,92},{32,9... | collective-permute-start | bytes 129032 | tf_op jit(solution)/shard_map/ppermute | solution.py:23
  589.4 28.0 %collective-permute-start.69 = (bf16[128,2048]{1,0:T(8,128)(2,1)S(1)}, bf16[128,2048]{1,0:T(8,128)(2,1)S(1)}, u32[]{:S(2)}, u32[]{:S(2)}) collective-permute-start(bf16[128,2048]{1,0:T(8,128)(2,1)S(1)} %copy-done.108), channel_id=1, source_target_pairs={{0,1},{1,0},{2,3},{3,2},{4,5},{5,4},{6,7},{7,6},{8,9},{9,8},{10,11... | collective-permute-start | bytes 1572872 | tf_op jit(solution)/shard_map/ppermute | solution.py:23
  633.7 24.0 %collective-permute-start.92 = (bf16[64,512]{1,0:T(8,128)(2,1)}, bf16[64,512]{1,0:T(8,128)(2,1)}, u32[]{:S(2)}, u32[]{:S(2)}) collective-permute-start(bf16[64,512]{1,0:T(8,128)(2,1)} %dynamic-slice_bitcast_fusion.53), channel_id=1, source_target_pairs={{0,16},{4,20},{8,24},{12,28},{16,0},{20,4},{24,8},{28,12},{32,48},... | collective-permute-start | bytes 196616 | tf_op jit(solution)/shard_map/ppermute | solution.py:23
  (271 other events, 2642.2 us)
